TPU v7x, 256 devices: a whole 4x4x8 slice. The times are simulated.
256 devices in a mesh: dp: 64 (over z, x_lo, y), mp: 4 (over x_hi, core).
Axes of the slice: x: 4 (x_hi: 2, x_lo: 2; x = x_hi * 2 + x_lo), y: 4, z: 8, core: 2. Of those that a mesh axis runs over, the one named last changes fastest.
Arguments:
- hidden_t: bfloat16 [29568, 8192], P(None, 'dp'), may hold values from -6 to 6
- cotangent: bfloat16 [8192, 4096], P('dp', 'mp'), may hold values from -0.0625 to 0.0625
- momentum: float32 [29568, 4096], P('dp', 'mp'), may hold values from -6 to 6
- basis: float32 [4096, 512], P('mp', 'dp'), may hold values from -0.09375 to 0.09375
Outputs:
- new_momentum: float32 [29568, 4096], P('dp', 'mp')
- new_basis: float32 [4096, 512], P('mp', 'dp')
- direction: bfloat16 [29568, 4096], P('dp', 'mp')
All inputs are finite; a program needn't handle non-finite values.
Results may differ from a plain program's by a relative error of at most 0.0015.
Values may be sent and summed in bfloat16 or wider, within the bound.
A program may use at most 320 MiB of HBM per device.

v0:
```python
import jax
import jax.numpy as jnp
from jax import lax
from jax.sharding import PartitionSpec as P

D = 4096
FF = 29568
RANK = 512


epsilon = 1e-06
momentum_rate = 0.95


def per_device(hidden_t, cotangent, momentum, basis):
    highest = lax.Precision.HIGHEST
    row_block = lax.all_to_all(hidden_t, "dp", split_axis=0, concat_axis=1, tiled=True)
    gradient = jnp.dot(
        row_block,
        lax.all_gather(cotangent, "dp", axis=0, tiled=True),
        preferred_element_type=jnp.float32,
    )
    whole_basis = lax.all_gather(basis, "dp", axis=1, tiled=True)
    merged = momentum + gradient
    left_prod = lax.psum(jnp.dot(merged, whole_basis, precision=highest), "mp")
    gram_sum = lax.psum(jnp.dot(left_prod.T, left_prod, precision=highest), "dp")
    factor = jnp.linalg.cholesky(gram_sum)
    orthonormal = jax.scipy.linalg.solve_triangular(factor, left_prod.T, lower=True).T
    right_part = jnp.dot(merged.T, orthonormal, precision=highest)
    rank_share = basis.shape[1]
    right_full = lax.psum(right_part, "dp")
    squares = lax.psum(jnp.sum(right_full * right_full, axis=0), "mp")
    unit_cols = right_full / (jnp.sqrt(squares) + epsilon)
    new_basis = lax.dynamic_slice_in_dim(
        unit_cols, lax.axis_index("dp") * rank_share, rank_share, 1
    )
    new_momentum = merged - (1.0 - momentum_rate) * jnp.dot(
        orthonormal, right_full.T, precision=highest
    )
    direction_scale = (FF * D / RANK) ** 0.5
    direction = (direction_scale * jnp.dot(orthonormal, unit_cols.T, precision=highest)).astype(
        jnp.bfloat16
    )
    return (new_momentum, new_basis, direction)


def solution(mesh):
    in_specs = (P(None, "dp"), P("dp", "mp"), P("dp", "mp"), P("mp", "dp"))
    out_specs = (P("dp", "mp"), P("mp", "dp"), P("dp", "mp"))
    return jax.shard_map(
        per_device, mesh=mesh, in_specs=in_specs, out_specs=out_specs, check_vma=False
    )
```

profile of v0, /device:TPU:1, one launch (start us, length us, event | category | flops | bytes accessed | tf_op | source)
XLA Modules:
  0.0 2230.0 jit_solution(17742726457962877496)
XLA Ops:
  7.2 0.7 all-gather.3.cloned.1.call-update
  7.9 9.1 all_to_all.14
  17.0 13.8 all-to-all-start
  30.9 0.7 all-gather.5.cloned.1.call-update
  31.6 216.3 %all-to-all-done = bf16[64,462,128]{2,1,0:T(8,128)(2,1)} async-done(((bf16[64,462,128]{2,1,0:T(8,128)(2,1)}), bf16[64,462,128]{2,1,0:T(8,128)(2,1)}, u32[]{:S(2)}, u32[]{:S(2)}) %all-to-all-start) | async-done | bytes 7569440 | tf_op jit(solution)/shard_map/all_to_all | solution.py:17
  248.0 8.2 copy.10
  256.2 5.0 pad.12
  261.2 29.3 %copy.15 = bf16[58,8,64,128]{3,1,2,0:T(8,128)(2,1)} copy(bf16[58,8,64,128]{3,2,1,0:T(8,128)(2,1)S(1)} %bitcast.62) | data formatting | bytes 15204352
  290.6 140.1 %all-gather.3.cloned.1.call-done = bf16[8192,1024]{1,0:T(8,128)(2,1)} async-done(((bf16[128,1024]{1,0:T(8,128)(2,1)}), bf16[8192,1024]{1,0:T(8,128)(2,1)}) %all-gather.3.cloned.1.call-update) | async-done | bytes 16777232 | tf_op jit(solution)/shard_map/all_gather | solution.py:20
  430.7 14.1 convolution_add_fusion
  444.9 269.9 %all-gather.5.cloned.1.call-done = f32[1024,512]{0,1:T(8,128)} async-done(((f32[1024,8]{0,1:T(8,128)}), f32[1024,512]{0,1:T(8,128)}) %all-gather.5.cloned.1.call-update) | async-done | bytes 2097168 | tf_op jit(solution)/shard_map/all_gather | solution.py:23
  714.8 5.7 fusion.35
  720.6 93.1 %all-reduce.5.cloned.1.call-done = f32[462,512]{1,0:T(8,128)} async-done(((f32[462,512]{1,0:T(8,128)}), f32[462,512]{1,0:T(8,128)}) %all-reduce.5.cloned.1.call-update) | async-done | bytes 946192 | tf_op jit(solution)/shard_map/psum | solution.py:25
  813.7 4.4 fusion.36
  818.1 0.4 all-reduce.9.cloned.1.call-start
  818.6 562.6 %all-reduce.7.cloned.1.call-done = f32[512,512]{0,1:T(8,128)} async-done(((f32[512,512]{0,1:T(8,128)}), f32[512,512]{0,1:T(8,128)}) %all-reduce.7.cloned.1.call-update) | async-done | bytes 1048592 | tf_op jit(solution)/shard_map/psum | solution.py:26
  1381.2 2.7 copy.12
  1383.9 1.4 fusion
  1385.3 1.0 copy-done.7
  1386.3 11.7 cholesky.104
  1398.1 9.8 custom-call.31
  1408.0 1.2 constant_dynamic-update-slice_fusion.3
  1409.3 1.3 convolution_subtract_fusion.3
  1410.5 11.7 cholesky.217
  1422.3 10.0 custom-call.32
  1432.5 1.0 copy-done.3
  1433.5 1.3 convolution_subtract_fusion.4
  1434.9 11.7 cholesky.238
  1446.6 0.6 select_reduce_fusion.1
  1447.2 0.6 compare_reduce_fusion.1
  1447.8 9.8 custom-call.33
  1457.7 0.8 convolution_dynamic-update-slice_fusion.1
  1458.5 1.4 convolution_subtract_fusion.5
  1459.9 11.7 cholesky.255
  1471.6 0.7 select_reduce_fusion
  1472.3 0.7 compare_reduce_fusion
  1473.0 0.7 compare_reduce_fusion.2
  1476.1 2.6 select_select_fusion
  1478.7 14.1 while.1
  1478.7 0.6 fusion.52
  1479.3 2.9 bitcast_dynamic-update-slice_fusion.2
  1482.3 0.6 fusion.52
  1482.9 2.9 bitcast_dynamic-update-slice_fusion.2
  1485.9 0.6 fusion.52
  1486.5 2.9 bitcast_dynamic-update-slice_fusion.2
  1489.4 0.6 fusion.52
  1490.0 2.8 bitcast_dynamic-update-slice_fusion.2
  1492.8 40.1 %custom-call.34 = f32[4,128,128]{1,2,0:T(8,128)S(1)} custom-call(f32[4,128,128]{2,1,0:T(8,128)} %get-tuple-element.10), custom_call_target="InvertDiagBlocksLowerTriangular" | custom-call | tf_op jit(solution)/shard_map/jit(_solve_triangular)/triangular_solve | solution.py:28
  1533.0 0.3 fusion.10
  1533.7 1.2 convolution_subtract_fusion.2
  1534.9 1.2 fusion.23
  1536.1 1.4 convolution_subtract_fusion.1
  1537.5 1.2 fusion.21
  1538.7 1.8 convolution_subtract_fusion
  1540.5 1.2 fusion.20
  1541.7 4.9 fusion.16
  1546.6 607.3 %all-reduce.9.cloned.1.call-done = f32[1024,512]{1,0:T(8,128)} async-done(((f32[1024,512]{1,0:T(8,128)}), f32[1024,512]{1,0:T(8,128)}) %all-reduce.9.cloned.1.call-update) | async-done | bytes 2097168 | tf_op jit(solution)/shard_map/psum | solution.py:31
  2153.9 2.0 multiply_reduce_fusion
  2155.9 53.0 %psum.31 = f32[512]{0:T(512)S(1)} all-reduce(f32[512]{0:T(512)S(1)} %multiply_reduce_fusion), channel_id=1, replica_groups=mesh['dp'=64,'mp'=4] {'mp'}, use_global_device_ids=true, to_apply=%region_12.13 | all-reduce | flops 512 | bytes 4096 | tf_op jit(solution)/shard_map/psum | solution.py:32
  2209.2 0.7 copy-done.5
  2209.9 4.2 multiply_convert_fusion
  2214.1 1.0 constant_dynamic-slice_fusion.1
  2215.1 1.8 copy.13
  2216.9 6.1 multiply_subtract_fusion
  (38 shorter events, 1.6 us)
Async XLA Ops:
  7.2 423.6 %all-gather.3.cloned.1.call-start = ((), (), s32[]{:S(2)}) async-start(), calls=%async_computation.1 | async-start | bytes 17039360 | tf_op jit(solution)/shard_map/all_gather | solution.py:20
  17.0 231.0 %all-to-all-start = ((bf16[64,462,128]{2,1,0:T(8,128)(2,1)}), bf16[64,462,128]{2,1,0:T(8,128)(2,1)}, u32[]{:S(2)}, u32[]{:S(2)}) async-start(bf16[64,462,128]{2,1,0:T(8,128)(2,1)} %all_to_all.14), calls=%async_computation | async-start | bytes 15204352 | tf_op jit(solution)/shard_map/all_to_all | solution.py:17
  30.8 684.0 %all-gather.5.cloned.1.call-start = ((), (), s32[]{:S(2)}) async-start(), calls=%async_computation.2 | async-start | bytes 2129920 | tf_op jit(solution)/shard_map/all_gather | solution.py:23
  31.6 782.1 %all-reduce.5.cloned.1.call-start = ((), (), s32[]{:S(2)}) async-start(), calls=%async_computation.3 | async-start | bytes 1900544 | tf_op jit(solution)/shard_map/psum | solution.py:25
  444.9 1096.9 %copy-start.1 = (f32[462,1024]{1,0:T(8,128)}, f32[462,1024]{1,0:T(8,128)S(1)}, u32[]{:S(2)}) copy-start(f32[462,1024]{1,0:T(8,128)S(1)} %convolution_add_fusion) | copy-start | bytes 5677060
  720.6 660.6 %all-reduce.7.cloned.1.call-start = ((), (), s32[]{:S(2)}) async-start(), calls=%async_computation.4 | async-start | bytes 2097152 | tf_op jit(solution)/shard_map/psum | solution.py:26
  818.1 1335.8 %all-reduce.9.cloned.1.call-start = ((), (), s32[]{:S(2)}) async-start(), calls=%async_computation.5 | async-start | bytes 4194304 | tf_op jit(solution)/shard_map/psum | solution.py:31
  1381.2 2.7 copy-start.6
  1385.3 1.0 copy-start.7
  1432.5 1.0 copy-start.3
  1434.8 98.1 %copy-start.2 = (f32[462,512]{1,0:T(8,128)S(1)}, f32[462,512]{1,0:T(8,128)}, u32[]{:S(2)}) copy-start(f32[462,512]{1,0:T(8,128)} %all-reduce.5.cloned.1.call-done) | copy-start | bytes 2838532
  1532.9 0.7 copy-start.8
  1538.7 3.0 copy-start.4
  2153.9 55.0 %copy-start = (f32[1024,512]{1,0:T(8,128)S(1)}, f32[1024,512]{1,0:T(8,128)}, u32[]{:S(2)}) copy-start(f32[1024,512]{1,0:T(8,128)} %all-reduce.9.cloned.1.call-done) | copy-start | bytes 6291460
  2208.9 0.9 copy-start.5
Sparse Core Ops, SparseCore 0:
  9.8 420.8 all-gather.2
  432.5 282.2 all-gather.4
  720.7 92.9 all-reduce.4
  818.2 562.9 all-reduce.6
  1546.8 607.1 all-reduce.8
where the time goes:
time: 2240 us; the launch traced here: 2230 us
  waiting for transfers between devices  1890 us (84%)
  other arithmetic  126 us (6%)
  local copies, waits for them, and re-layouts  74.5 us (3%)
  matrix products  54.1 us (2%)
  blocking collectives  53 us (2%)
    psum x1, waiting for transfers between devices, per_device(): right_full = lax.psum(right_part, 'dp')  607 us
    psum x1, waiting for transfers between devices, per_device(): lax.psum(jnp.dot(left_prod.T, left_prod, precision=highest), 'dp')  563 us
    all_gather x1, waiting for transfers between devices, per_device(): whole_basis = lax.all_gather(basis, 'dp', axis=1, tiled=True)  270 us
    all_to_all x1, waiting for transfers between devices, per_device(): lax.all_to_all(hidden_t, 'dp', split_axis=0, concat_axis=1, tiled=True)  216 us
    all_gather x1, waiting for transfers between devices, per_device(): lax.all_gather(cotangent, 'dp', axis=0, tiled=True)  140 us
    psum x1, waiting for transfers between devices, per_device(): left_prod = lax.psum(jnp.dot(merged, whole_basis, precision=highest), 'mp')  93.1 us
    another operation x14, other arithmetic, per_device(): factor = jnp.linalg.cholesky(gram_sum)  79.8 us
    psum x1, blocking collectives, per_device(): squares = lax.psum(jnp.sum(right_full * right_full, axis=0), 'mp')  53 us
  transfers between devices with their start and end apart: 6, of which 6 were waited for; matrix products, arithmetic and copies ran while one was open for 3% of the time, Pallas kernels for 0%

commit v1 on v0

--- a/solution.py
+++ b/solution.py
@@ -1,15 +1,122 @@
 import jax
 import jax.numpy as jnp
 from jax import lax
+from jax.experimental import pallas as pl
+from jax.experimental.pallas import tpu as pltpu
 from jax.sharding import PartitionSpec as P
 
 D = 4096
 FF = 29568
 RANK = 512
 
+NY, NXL, NZ = 4, 2, 8
 
 epsilon = 1e-06
 momentum_rate = 0.95
+
+
+def place():
+    dp = lax.axis_index("dp")
+    return dp // (NXL * NY), (dp // NY) % NXL, dp % NY
+
+
+def dp_of(z, xl, y):
+    return (z * NXL + xl) * NY + y
+
+
+def greet(partners):
+    barrier = pltpu.get_barrier_semaphore()
+    for device in partners:
+        pl.semaphore_signal(
+            barrier, inc=1, device_id=device, device_id_type=pl.DeviceIdType.MESH
+        )
+    pl.semaphore_wait(barrier, len(partners))
+
+
+def send(src, dst, send_sem, recv_sem, device):
+    copy = pltpu.make_async_remote_copy(
+        src_ref=src,
+        dst_ref=dst,
+        send_sem=send_sem,
+        recv_sem=recv_sem,
+        device_id=device,
+        device_id_type=pl.DeviceIdType.MESH,
+    )
+    copy.start()
+    return copy
+
+
+def sum_kernel(in_ref, out_ref, buf_y, buf_x, buf_z, acc_y, acc_x, send_sems, recv_sems):
+    z, xl, y = place()
+    rows = in_ref.shape[0]
+    ry, rx, rz = rows // NY, rows // (NY * NXL), rows // (NY * NXL * NZ)
+    to_y = [{"dp": dp_of(z, xl, (y + k) % NY)} for k in range(1, NY)]
+    to_x = {"dp": dp_of(z, 1 - xl, y)}
+    to_z = [{"dp": dp_of((z + k) % NZ, xl, y)} for k in range(1, NZ)]
+    greet(to_y + [to_x] + to_z)
+
+    sem = iter(range(22))
+
+    def start(src, dst, device):
+        s = next(sem)
+        return send(src, dst, send_sems.at[s], recv_sems.at[s], device)
+
+    copies = [
+        start(in_ref.at[pl.ds(((y + k) % NY) * ry, ry)], buf_y.at[k - 1], to_y[k - 1])
+        for k in range(1, NY)
+    ]
+    acc_y[...] = in_ref[pl.ds(y * ry, ry), :]
+    for copy in copies:
+        copy.wait()
+    acc_y[...] += buf_y[0] + buf_y[1] + buf_y[2]
+
+    copy = start(acc_y.at[pl.ds((1 - xl) * rx, rx)], buf_x, to_x)
+    copy.wait()
+    acc_x[...] = acc_y[pl.ds(xl * rx, rx), :] + buf_x[...]
+
+    copies = [
+        start(acc_x.at[pl.ds(((z + k) % NZ) * rz, rz)], buf_z.at[k - 1], to_z[k - 1])
+        for k in range(1, NZ)
+    ]
+    total = acc_x[pl.ds(z * rz, rz), :]
+    for k in range(NZ - 1):
+        copies[k].wait()
+        total = total + buf_z[k]
+    base = y * ry + xl * rx
+    mine = out_ref.at[pl.ds(base + z * rz, rz)]
+    out_ref[pl.ds(base + z * rz, rz), :] = total
+    copies = [start(mine, mine, to_z[k]) for k in range(NZ - 1)]
+    for copy in copies:
+        copy.wait()
+    mine = out_ref.at[pl.ds(base, rx)]
+    start(mine, mine, to_x).wait()
+    mine = out_ref.at[pl.ds(y * ry, ry)]
+    copies = [start(mine, mine, to_y[k]) for k in range(NY - 1)]
+    for copy in copies:
+        copy.wait()
+
+
+def sum_over_dp(x):
+    rows, cols = x.shape
+    f32 = jnp.float32
+    return pl.pallas_call(
+        sum_kernel,
+        out_shape=jax.ShapeDtypeStruct(x.shape, f32),
+        in_specs=[pl.BlockSpec(memory_space=pltpu.VMEM)],
+        out_specs=pl.BlockSpec(memory_space=pltpu.VMEM),
+        scratch_shapes=[
+            pltpu.VMEM((NY - 1, rows // NY, cols), f32),
+            pltpu.VMEM((rows // (NY * NXL), cols), f32),
+            pltpu.VMEM((NZ - 1, rows // (NY * NXL * NZ), cols), f32),
+            pltpu.VMEM((rows // NY, cols), f32),
+            pltpu.VMEM((rows // (NY * NXL), cols), f32),
+            pltpu.SemaphoreType.DMA((22,)),
+            pltpu.SemaphoreType.DMA((22,)),
+        ],
+        compiler_params=pltpu.CompilerParams(
+            collective_id=1, has_side_effects=True, vmem_limit_bytes=40 << 20
+        ),
+    )(x)
 
 
 def per_device(hidden_t, cotangent, momentum, basis):
@@ -20,15 +127,20 @@
         lax.all_gather(cotangent, "dp", axis=0, tiled=True),
         preferred_element_type=jnp.float32,
     )
-    whole_basis = lax.all_gather(basis, "dp", axis=1, tiled=True)
+    whole_basis = lax.all_gather(basis.T, "dp", axis=0, tiled=True).T
     merged = momentum + gradient
     left_prod = lax.psum(jnp.dot(merged, whole_basis, precision=highest), "mp")
-    gram_sum = lax.psum(jnp.dot(left_prod.T, left_prod, precision=highest), "dp")
+    gram_part = jnp.dot(left_prod.T, left_prod, precision=highest)
+    right_part = jnp.dot(merged.T, left_prod, precision=highest)
+    sums = sum_over_dp(jnp.concatenate([right_part, gram_part], axis=0))
+    gram_sum = sums[1024:]
     factor = jnp.linalg.cholesky(gram_sum)
-    orthonormal = jax.scipy.linalg.solve_triangular(factor, left_prod.T, lower=True).T
-    right_part = jnp.dot(merged.T, orthonormal, precision=highest)
+    inverse = jax.scipy.linalg.solve_triangular(
+        factor, jnp.eye(RANK, dtype=jnp.float32), lower=True
+    )
+    orthonormal = jnp.dot(left_prod, inverse.T, precision=highest)
     rank_share = basis.shape[1]
-    right_full = lax.psum(right_part, "dp")
+    right_full = jnp.dot(sums[:1024], inverse.T, precision=highest)
     squares = lax.psum(jnp.sum(right_full * right_full, axis=0), "mp")
     unit_cols = right_full / (jnp.sqrt(squares) + epsilon)
     new_basis = lax.dynamic_slice_in_dim(

time: 2240 us -> 1140 us (0.51)
  waiting for transfers between devices: 1890 us -> 730 us
  Pallas kernels: 0 us -> 112 us
  blocking collectives: 53 us -> 10.1 us
    psum x2 -> x0, waiting for transfers between devices: 1170 us -> none  [the longest x1 607 us: per_device(): right_full = lax.psum(right_part, 'dp')]
    pallas_call x0 -> x1, Pallas kernels: none -> 112 us  [sum_over_dp(): pl.pallas_call(sum_kernel, out_shape=jax.ShapeDtypeStruct(x.shape, f32),...]
    psum x1, blocking collectives: 53 us -> 10.1 us  [per_device(): squares = lax.psum(jnp.sum(right_full * right_full, axis=0), 'mp')]
  transfers between devices with their start and end apart: 6 -> 4, of which waited for: 6 -> 4; matrix products, arithmetic and copies ran while one was open for 3% -> 4% of each run, Pallas kernels for 0% -> 0%
where the time goes in v1:
time: 1140 us; the launch traced here: 1130 us
  waiting for transfers between devices  730 us (64%)
  other arithmetic  130 us (11%)
  Pallas kernels  112 us (10%)
  local copies, waits for them, and re-layouts  61.5 us (5%)
  matrix products  58 us (5%)
  between operations  16.8 us (1%)
  starting transfers between devices  13.9 us (1%)
    all_gather x1, waiting for transfers between devices, per_device(): whole_basis = lax.all_gather(basis.T, 'dp', axis=0, tiled=True).T  270 us
    all_to_all x1, waiting for transfers between devices, per_device(): lax.all_to_all(hidden_t, 'dp', split_axis=0, concat_axis=1, tiled=True)  217 us
    all_gather x1, waiting for transfers between devices, per_device(): lax.all_gather(cotangent, 'dp', axis=0, tiled=True)  151 us
    pallas_call x1, Pallas kernels, sum_over_dp(): pl.pallas_call(sum_kernel, out_shape=jax.ShapeDtypeStruct(x.shape, f32),...  112 us
    psum x1, waiting for transfers between devices, per_device(): left_prod = lax.psum(jnp.dot(merged, whole_basis, precision=highest), 'mp')  91.2 us
    another operation x14, other arithmetic, per_device(): factor = jnp.linalg.cholesky(gram_sum)  80.8 us
    another operation x3, other arithmetic, per_device(): jax.scipy.linalg.solve_triangular(factor, jnp.eye(RANK, dtype=jnp.float32...  43.3 us
    unnamed x29, local copies, waits for them, and re-layouts  27.3 us
  transfers between devices with their start and end apart: 4, of which 4 were waited for; matrix products, arithmetic and copies ran while one was open for 4% of the time, Pallas kernels for 0%

profile of v1, /device:TPU:1, one launch (start us, length us, event | category | flops | bytes accessed | tf_op | source)
XLA Modules:
  0.0 1132.7 jit_solution(8282487147717315946)
XLA Ops:
  7.2 0.7 all-gather.3.cloned.1.call-update
  7.9 9.1 all_to_all.14
  17.0 13.8 %all-to-all-start = ((bf16[64,462,128]{2,1,0:T(8,128)(2,1)}), bf16[64,462,128]{2,1,0:T(8,128)(2,1)}, u32[]{:S(2)}, u32[]{:S(2)}) async-start(bf16[64,462,128]{2,1,0:T(8,128)(2,1)} %all_to_all.14), calls=%async_computation | async-start | bytes 15204352 | tf_op jit(solution)/shard_map/all_to_all | solution.py:124
  30.9 0.7 all-gather.5.cloned.1.call-update
  31.6 216.9 %all-to-all-done = bf16[64,462,128]{2,1,0:T(8,128)(2,1)} async-done(((bf16[64,462,128]{2,1,0:T(8,128)(2,1)}), bf16[64,462,128]{2,1,0:T(8,128)(2,1)}, u32[]{:S(2)}, u32[]{:S(2)}) %all-to-all-start) | async-done | bytes 7569440 | tf_op jit(solution)/shard_map/all_to_all | solution.py:124
  248.6 8.2 copy.9
  256.8 5.0 pad.14
  261.8 18.6 %copy.13 = bf16[58,8,64,128]{3,1,2,0:T(8,128)(2,1)} copy(bf16[58,8,64,128]{3,2,1,0:T(8,128)(2,1)S(1)} %bitcast.66) | data formatting | bytes 15204352
  280.5 150.6 %all-gather.3.cloned.1.call-done = bf16[8192,1024]{1,0:T(8,128)(2,1)} async-done(((bf16[128,1024]{1,0:T(8,128)(2,1)}), bf16[8192,1024]{1,0:T(8,128)(2,1)}) %all-gather.3.cloned.1.call-update) | async-done | bytes 16777232 | tf_op jit(solution)/shard_map/all_gather | solution.py:127
  431.1 14.3 %convolution_add_fusion = f32[462,1024]{1,0:T(8,128)S(1)} fusion(f32[462,1024]{1,0:T(8,128)} %param.6, bf16[462,8192]{1,0:T(8,128)(2,1)} %bitcast.67, bf16[8192,1024]{1,0:T(8,128)(2,1)} %all-gather.3.cloned.1.call-done), kind=kOutput, calls=%fused_computation.8 | convolution fusion | flops 7751546880 | bytes 28131328 | tf_op jit(solution)/shard_map/dot_general | solution.py:125
  445.4 270.0 %all-gather.5.cloned.1.call-done = f32[512,1024]{1,0:T(8,128)} async-done(((f32[8,1024]{1,0:T(8,128)}), f32[512,1024]{1,0:T(8,128)}) %all-gather.5.cloned.1.call-update) | async-done | bytes 2097168 | tf_op jit(solution)/shard_map/all_gather | solution.py:130
  715.4 5.7 fusion.37
  721.2 0.8 iota_compare_fusion
  722.0 1.1 fusion.12
  723.1 91.2 %all-reduce.3.cloned.1.call-done = f32[462,512]{1,0:T(8,128)} async-done(((f32[462,512]{1,0:T(8,128)}), f32[462,512]{1,0:T(8,128)}) %all-reduce.3.cloned.1.call-update) | async-done | bytes 946192 | tf_op jit(solution)/shard_map/psum | solution.py:132
  814.3 4.8 fusion.38
  819.1 2.0 fusion.39
  821.4 112.5 %shard_map.67 = f32[1536,512]{1,0:T(8,128)S(1)} custom-call(f32[1536,512]{1,0:T(8,128)S(1)} %pad_maximum_fusion.in_ref), custom_call_target="tpu_custom_call" | custom-call | tf_op jit(solution)/shard_map/pallas_call | solution.py:102
  933.9 1.1 slice.120
  935.0 2.6 copy.12
  937.6 1.4 fusion.2
  939.0 1.0 copy-done.9
  940.1 11.9 %cholesky.104 = f32[128,128]{1,0:T(8,128)S(1)} custom-call(f32[128,128]{1,0:T(8,128)S(1)} %cholesky.266), custom_call_target="Cholesky" | custom-call | tf_op jit(solution)/shard_map/jit(cholesky)/cholesky | solution.py:137
  952.0 9.8 custom-call.31
  961.8 1.1 cholesky.224
  963.0 1.9 constant_dynamic-update-slice_fusion.3
  964.9 1.2 convolution_subtract_fusion.3
  966.1 11.7 %cholesky.217 = f32[128,128]{1,0:T(8,128)S(1)} custom-call(f32[128,128]{1,0:T(8,128)S(1)} %cholesky.270), custom_call_target="Cholesky" | custom-call | tf_op jit(solution)/shard_map/jit(cholesky)/cholesky | solution.py:137
  977.9 0.7 select_reduce_fusion.2
  978.5 9.8 custom-call.32
  988.3 1.0 convolution_dynamic-update-slice_fusion
  989.3 1.4 convolution_subtract_fusion.4
  990.7 12.1 %cholesky.238 = f32[128,128]{1,0:T(8,128)S(1)} custom-call(f32[128,128]{1,0:T(8,128)S(1)} %cholesky.275), custom_call_target="Cholesky" | custom-call | tf_op jit(solution)/shard_map/jit(cholesky)/cholesky | solution.py:137
  1002.8 0.7 select_reduce_fusion.1
  1003.5 0.7 compare_reduce_fusion.1
  1004.2 9.8 custom-call.33
  1014.0 0.8 convolution_dynamic-update-slice_fusion.1
  1014.8 1.4 convolution_subtract_fusion.5
  1016.2 11.7 %cholesky.255 = f32[128,128]{1,0:T(8,128)S(1)} custom-call(f32[128,128]{1,0:T(8,128)S(1)} %convolution_subtract_fusion.5), custom_call_target="Cholesky" | custom-call | tf_op jit(solution)/shard_map/jit(cholesky)/cholesky | solution.py:137
  1027.9 0.7 select_reduce_fusion
  1028.6 0.6 compare_reduce_fusion
  1029.2 0.7 compare_reduce_fusion.2
  1032.4 2.4 select_select_fusion
  1034.8 14.0 %while.1 = (s32[]{:T(128)}, f32[512,512]{1,0:T(8,128)}, s32[4,2]{0,1:T(2,128)S(1)}, f32[4,128,128]{2,1,0:T(8,128)}, s32[]{:T(128)}) while((s32[]{:T(128)}, f32[512,512]{1,0:T(8,128)}, s32[4,2]{0,1:T(2,128)S(1)}, f32[4,128,128]{2,1,0:T(8,128)}, s32[]{:T(128)}) %tuple.32), condition=%wide.while_cond, body=%wide.while_body.sunk | while | flops 2 | bytes 132705 | solution.py:138
  1034.8 0.5 fusion.59
  1035.4 2.9 bitcast_dynamic-update-slice_fusion.2
  1038.3 0.5 fusion.59
  1038.9 2.9 bitcast_dynamic-update-slice_fusion.2
  1041.8 0.5 fusion.59
  1042.4 2.9 bitcast_dynamic-update-slice_fusion.2
  1045.9 2.8 bitcast_dynamic-update-slice_fusion.2
  1048.7 40.9 %custom-call.34 = f32[4,128,128]{1,2,0:T(8,128)} custom-call(f32[4,128,128]{2,1,0:T(8,128)} %get-tuple-element.10), custom_call_target="InvertDiagBlocksLowerTriangular" | custom-call | tf_op jit(solution)/shard_map/jit(_solve_triangular)/triangular_solve | solution.py:138
  1089.6 1.2 fusion.14
  1090.9 1.4 convolution_subtract_fusion.1
  1092.2 1.3 fusion.26
  1093.5 1.5 convolution_subtract_fusion
  1095.5 1.8 convolution_subtract_fusion.2
  1097.7 4.9 multiply_reduce_fusion
  1102.6 10.1 psum.15
  1112.8 2.0 broadcast_divide_fusion
  1114.8 1.7 fusion.8
  1116.5 4.6 multiply_subtract_fusion
  1121.1 4.2 multiply_convert_fusion
  1125.3 0.6 constant_dynamic-slice_fusion.1
  (45 shorter events, 2.3 us)
Async XLA Ops:
  7.2 423.9 %all-gather.3.cloned.1.call-start = ((), (), s32[]{:S(2)}) async-start(), calls=%async_computation.1 | async-start | bytes 17039360 | tf_op jit(solution)/shard_map/all_gather | solution.py:127
  17.0 231.5 %all-to-all-start = ((bf16[64,462,128]{2,1,0:T(8,128)(2,1)}), bf16[64,462,128]{2,1,0:T(8,128)(2,1)}, u32[]{:S(2)}, u32[]{:S(2)}) async-start(bf16[64,462,128]{2,1,0:T(8,128)(2,1)} %all_to_all.14), calls=%async_computation | async-start | bytes 15204352 | tf_op jit(solution)/shard_map/all_to_all | solution.py:124
  30.8 684.6 %all-gather.5.cloned.1.call-start = ((), (), s32[]{:S(2)}) async-start(), calls=%async_computation.2 | async-start | bytes 2129920 | tf_op jit(solution)/shard_map/all_gather | solution.py:130
  31.6 782.7 %all-reduce.3.cloned.1.call-start = ((), (), s32[]{:S(2)}) async-start(), calls=%async_computation.3 | async-start | bytes 1900544 | tf_op jit(solution)/shard_map/psum | solution.py:132
  445.4 368.9 %copy-start.1 = (f32[462,1024]{1,0:T(8,128)}, f32[462,1024]{1,0:T(8,128)S(1)}, u32[]{:S(2)}) copy-start(f32[462,1024]{1,0:T(8,128)S(1)} %convolution_add_fusion) | copy-start | bytes 5677060
  814.3 4.9 copy-start.3
  939.0 1.0 copy-start.9
  1089.6 5.4 copy-start.12
  1093.5 9.1 copy-start.5
  1095.5 7.1 copy-start.7
  1097.7 4.9 copy-start.10
  1112.7 2.0 copy-start.4
  1112.7 2.0 copy-start.6
  1112.7 2.0 copy-start.8
  1112.7 2.0 copy-start.11
  1112.7 3.8 copy-start.2
  1114.8 1.8 copy-start
Sparse Core Ops, SparseCore 0:
  9.8 421.2 all-gather.2
  432.9 282.5 all-gather.4
  721.3 92.9 all-reduce.2

commit v2 on v1

--- a/solution.py
+++ b/solution.py
@@ -119,25 +119,305 @@
     )(x)
 
 
+ROWS = 462
+HROWS = 480
+HALF = HROWS // 2
+BLOCKS = 4
+BCOLS = 1024 // BLOCKS
+N_SEMS = 300
+
+
+def run_tasks(tasks):
+    tasks = list(tasks)
+    while tasks:
+        for task in list(tasks):
+            if next(task, "end") == "end":
+                tasks.remove(task)
+
+
+def grad_kernel(
+    hid, cot, mom, basis, out, whole, H, za, C, part, came, send_sems, recv_sems, local_sem
+):
+    z, xl, y = place()
+    mp = lax.axis_index("mp")
+    xh, core = mp // 2, mp % 2
+    z_dev = [{"dp": dp_of((z + k) % NZ, xl, y)} for k in range(NZ)]
+    y_dev = [{"dp": dp_of(z, xl, (y + k) % NY)} for k in range(NY)]
+    xl_dev = {"dp": dp_of(z, 1 - xl, y)}
+    xh_dev = {"mp": (mp + 2) % 4}
+    core_dev = {"mp": mp + 1 - 2 * core}
+    greet(z_dev[1:] + y_dev[1:] + [xl_dev, xh_dev, core_dev])
+
+    count = iter(range(N_SEMS))
+    started = []
+
+    def start(src, dst, device):
+        s = next(count)
+        copy = send(src, dst, send_sems.at[s], recv_sems.at[s], device)
+        started.append(copy)
+        return copy
+
+    my_rows = pl.ds(pl.multiple_of(xh * HALF, 16), HALF)
+    other_rows = pl.ds(pl.multiple_of((1 - xh) * HALF, 16), HALF)
+
+    def lanes(zs, ys):
+        return pl.ds(pl.multiple_of((zs * NY + ys) * 128, 128), 128)
+
+    def group(zs):
+        return pl.ds(pl.multiple_of(zs * 512, 512), 512)
+
+    def hid_chunk(zd, yd):
+        return hid.at[(zd * NXL + core) * NY + yd, my_rows, :]
+
+    def hidden_task():
+        mine = H.at[core, my_rows, lanes(z, y)]
+        by_y = {0: [start(hid_chunk(z, (y + j) % NY), mine, y_dev[j]) for j in (1, 3, 2)]}
+        by_z = {}
+        order = (1, 7, 2, 6, 3, 5, 4)
+        for k in order:
+            zd = (z + k) % NZ
+            by_z[k] = [start(hid_chunk(zd, y), mine, z_dev[k])] + [
+                start(hid_chunk(zd, (y + j) % NY), za.at[z, j - 1], z_dev[k]) for j in (1, 3, 2)
+            ]
+        local = pltpu.make_async_copy(hid_chunk(z, y), mine, local_sem)
+        local.start()
+        local.wait()
+        yield
+        x_copies, c_copies = {}, []
+
+        def finish(k):
+            for copy in by_y[k]:
+                copy.wait_recv()
+            ref = H.at[core, my_rows, group((z - k + NZ) % NZ)]
+            x_copies[k] = start(ref, ref, xh_dev)
+            c_copies.append(start(ref, ref, core_dev))
+
+        def cross(k):
+            x_copies[k].wait_recv()
+            ref = H.at[core, other_rows, group((z - k + NZ) % NZ)]
+            c_copies.append(start(ref, ref, core_dev))
+
+        seq = (0,) + order
+        for i, k in enumerate(order):
+            for copy in by_z[k]:
+                copy.wait_recv()
+            zs = (z - k + NZ) % NZ
+            there = H.at[core, my_rows, lanes(zs, y)]
+            by_y[k] = [start(za.at[zs, j - 1], there, y_dev[j]) for j in (1, 3, 2)]
+            yield
+            finish(seq[i])
+            if i:
+                cross(seq[i - 1])
+            yield
+        finish(seq[-1])
+        cross(seq[-2])
+        yield
+        cross(seq[-1])
+        for copy in c_copies:
+            copy.wait_recv()
+
+    def shard(b, zs, ys, half=None):
+        first = (zs * NY + ys) * 128
+        size = 128
+        if half is not None:
+            first, size = first + half * 64, 64
+        return C.at[b, pl.ds(pl.multiple_of(first, 64), size), :]
+
+    def gather_task(b):
+        own = cot.at[:, pl.ds(b * BCOLS, BCOLS)]
+        mine = shard(b, z, y)
+        right, left = start(own, mine, z_dev[1]), start(own, mine, z_dev[NZ - 1])
+        pushed = [(z, start(own, mine, y_dev[1]), start(own, mine, y_dev[3]))]
+        C[b, pl.ds(pl.multiple_of((z * NY + y) * 128, 128), 128), :] = cot[:, b * BCOLS : (b + 1) * BCOLS]
+        last = []
+
+        def forward():
+            for zi, up, down in pushed:
+                up.wait_recv()
+                ref = shard(b, zi, (y + 3) % NY, 0)
+                last.append(start(ref, ref, y_dev[1]))
+                down.wait_recv()
+                ref = shard(b, zi, (y + 1) % NY, 1)
+                last.append(start(ref, ref, y_dev[3]))
+
+        for t in range(1, 5):
+            yield
+            right.wait_recv()
+            left.wait_recv()
+            low, high = (z - t + NZ) % NZ, (z + t) % NZ
+            if t < 4:
+                half = (0, 1) if t == 3 else (None, None)
+                ref = shard(b, low, y, half[0])
+                right = start(ref, ref, z_dev[1])
+                ref = shard(b, high, y, half[1])
+                left = start(ref, ref, z_dev[NZ - 1])
+            now = []
+            for zi in (low, high) if t < 4 else (low,):
+                ref = shard(b, zi, y)
+                now.append((zi, start(ref, ref, y_dev[1]), start(ref, ref, y_dev[3])))
+            yield
+            forward()
+            pushed = now
+        yield
+        forward()
+        yield
+        for copy in last:
+            copy.wait_recv()
+
+    def basis_task():
+        def rows_of(zs, xs, ys, n):
+            return whole.at[pl.ds(pl.multiple_of(dp_of(zs, xs, ys) * 8, 8), n * 8), :]
+
+        mine = rows_of(z, xl, y, 1)
+        copies = [start(basis, mine, y_dev[j]) for j in (1, 3, 2)]
+        whole[pl.ds(pl.multiple_of(dp_of(z, xl, y) * 8, 8), 8), :] = basis[...]
+        yield
+        for copy in copies:
+            copy.wait_recv()
+        mine = rows_of(z, xl, 0, NY)
+        copies = {k: start(mine, mine, z_dev[k]) for k in (1, 7, 2, 6, 3, 5, 4)}
+        across = [start(mine, mine, xl_dev)]
+        for k, copy in copies.items():
+            yield
+            copy.wait_recv()
+            ref = rows_of((z - k + NZ) % NZ, xl, 0, NY)
+            across.append(start(ref, ref, xl_dev))
+        yield
+        yield
+        for copy in across:
+            copy.wait_recv()
+
+    def product(b, rows):
+        def step(kk, acc):
+            k = pl.ds(pl.multiple_of(kk * 512, 512), 512)
+            return acc + jnp.dot(H[rows, :, k], C[b, k, :], preferred_element_type=jnp.float32)
+
+        return lax.fori_loop(0, 8, step, jnp.zeros((HROWS, BCOLS), jnp.float32))
+
+    cross = []
+
+    def multiply(b):
+        part[b] = product(b, 1 - xl)
+        cross.append(start(part.at[b], came.at[b], xl_dev))
+        cols = slice(b * BCOLS, (b + 1) * BCOLS)
+        out[:, cols] = mom[:, cols] + product(b, xl)[:ROWS]
+
+    run_tasks([gather_task(b) for b in range(BLOCKS)] + [hidden_task(), basis_task()])
+    for b in range(BLOCKS):
+        multiply(b)
+        if b:
+            cross[b - 1].wait_recv()
+            cols = slice((b - 1) * BCOLS, b * BCOLS)
+            out[:, cols] += came[b - 1, :ROWS]
+    cross[-1].wait_recv()
+    cols = slice((BLOCKS - 1) * BCOLS, BLOCKS * BCOLS)
+    out[:, cols] += came[BLOCKS - 1, :ROWS]
+    for copy in started:
+        copy.wait_send()
+
+
+def merged_and_basis(hidden_t, cotangent, momentum, basis):
+    bf16, f32 = jnp.bfloat16, jnp.float32
+    hid = jnp.pad(hidden_t.reshape(64, ROWS, 128), ((0, 0), (0, HROWS - ROWS), (0, 0)))
+    vmem = pl.BlockSpec(memory_space=pltpu.VMEM)
+    return pl.pallas_call(
+        grad_kernel,
+        out_shape=(
+            jax.ShapeDtypeStruct((ROWS, 1024), f32),
+            jax.ShapeDtypeStruct((RANK, 1024), f32),
+        ),
+        in_specs=[pl.BlockSpec(memory_space=pl.ANY), vmem, vmem, vmem],
+        out_specs=(vmem, vmem),
+        scratch_shapes=[
+            pltpu.VMEM((2, HROWS, 4096), bf16),
+            pltpu.VMEM((NZ, NY - 1, HALF, 128), bf16),
+            pltpu.VMEM((BLOCKS, 4096, BCOLS), bf16),
+            pltpu.VMEM((BLOCKS, HROWS, BCOLS), f32),
+            pltpu.VMEM((BLOCKS, HROWS, BCOLS), f32),
+            pltpu.SemaphoreType.DMA((N_SEMS,)),
+            pltpu.SemaphoreType.DMA((N_SEMS,)),
+            pltpu.SemaphoreType.DMA,
+        ],
+        compiler_params=pltpu.CompilerParams(
+            collective_id=2, has_side_effects=True, vmem_limit_bytes=56 << 20
+        ),
+    )(hid, cotangent, momentum, basis.T)
+
+
+PB = 16
+
+def tdot(a, b):
+    return lax.dot_general(a, b, (((0,), (0,)), ((), ())), precision=lax.Precision.HIGHEST, preferred_element_type=jnp.float32)
+
+def eliminate(R0, R1, first):
+    n = R0.shape[0]
+    row_id = lax.broadcasted_iota(jnp.int32, (n, 128), 0)
+    cols = [jnp.broadcast_to(R0[:, first + m : first + m + 1], (n, 128)) for m in range(n)]
+    pivots = jnp.ones((n, 128), jnp.float32)
+    for j in range(n):
+        d = jnp.broadcast_to(cols[j][j : j + 1, :], (n, 128))
+        pivots = jnp.where(row_id == j, d, pivots)
+        if j + 1 < n:
+            f = jnp.where(row_id > j, cols[j], 0.0) * (1.0 / d)
+            for m in range(j + 1, n):
+                cols[m] = cols[m] - f * cols[m][j : j + 1, :]
+            R0 = R0 - f * R0[j : j + 1, :]
+            R1 = R1 - f * R1[j : j + 1, :]
+    scale = 1.0 / jnp.sqrt(pivots)
+    return R0 * scale, R1 * scale
+
+def factor_panel(S, work, p):
+    rows = pl.ds(p * 128, 128)
+    work[:, :128] = S[rows, p * 128 : p * 128 + 128]
+    r = lax.broadcasted_iota(jnp.int32, (128, 128), 0)
+    c = lax.broadcasted_iota(jnp.int32, (128, 128), 1)
+    work[:, 128:] = jnp.where(r == c, 1.0, 0.0).astype(jnp.float32)
+    for b in range(128 // PB):
+        lo = b * PB
+        u0, u1 = eliminate(work[lo : lo + PB, :128], work[lo : lo + PB, 128:], lo)
+        work[lo : lo + PB, 128:] = u1
+        if b + 1 < 128 // PB:
+            u = jnp.concatenate([u0, u1], axis=1)
+            upd = tdot(u0, u)
+            work[lo + PB :, :] = work[lo + PB :, :] - upd[lo + PB :, :]
+
+def panel_step(S, work, p):
+    factor_panel(S, work, p)
+    rows = slice(p * 128, p * 128 + 128)
+    end = 512 + (p + 1) * 128
+    start = p * 128
+    u = jnp.dot(work[:, 128:], S[rows, start:end], precision=lax.Precision.HIGHEST, preferred_element_type=jnp.float32)
+    S[rows, start:end] = u
+    if p < 3:
+        tr = tdot(u[:, 128 : 512 - start], u[:, 128:])
+        S[(p + 1) * 128 : 512, start + 128 : end] = S[(p + 1) * 128 : 512, start + 128 : end] - tr
+
+def factor_kernel(a, x, S, work):
+    S[:, :512] = a[...]
+    r = lax.broadcasted_iota(jnp.int32, (512, 512), 0)
+    c = lax.broadcasted_iota(jnp.int32, (512, 512), 1)
+    S[:, 512:] = jnp.where(r == c, 1.0, 0.0).astype(jnp.float32)
+    for p in range(4):
+        panel_step(S, work, p)
+    x[...] = S[:, 512:]
+
+def inv_factor(a):
+    return pl.pallas_call(factor_kernel, out_shape=jax.ShapeDtypeStruct((512, 512), jnp.float32),
+        in_specs=[pl.BlockSpec(memory_space=pltpu.VMEM)], out_specs=pl.BlockSpec(memory_space=pltpu.VMEM),
+        scratch_shapes=[pltpu.VMEM((512, 1024), jnp.float32), pltpu.VMEM((128, 256), jnp.float32)],
+        compiler_params=pltpu.CompilerParams(vmem_limit_bytes=40 << 20))(a)
+
+
 def per_device(hidden_t, cotangent, momentum, basis):
     highest = lax.Precision.HIGHEST
-    row_block = lax.all_to_all(hidden_t, "dp", split_axis=0, concat_axis=1, tiled=True)
-    gradient = jnp.dot(
-        row_block,
-        lax.all_gather(cotangent, "dp", axis=0, tiled=True),
-        preferred_element_type=jnp.float32,
-    )
-    whole_basis = lax.all_gather(basis.T, "dp", axis=0, tiled=True).T
-    merged = momentum + gradient
+    merged, basis_rows = merged_and_basis(hidden_t, cotangent, momentum, basis)
+    whole_basis = basis_rows.T
     left_prod = lax.psum(jnp.dot(merged, whole_basis, precision=highest), "mp")
     gram_part = jnp.dot(left_prod.T, left_prod, precision=highest)
     right_part = jnp.dot(merged.T, left_prod, precision=highest)
     sums = sum_over_dp(jnp.concatenate([right_part, gram_part], axis=0))
     gram_sum = sums[1024:]
-    factor = jnp.linalg.cholesky(gram_sum)
-    inverse = jax.scipy.linalg.solve_triangular(
-        factor, jnp.eye(RANK, dtype=jnp.float32), lower=True
-    )
+    inverse = inv_factor(gram_sum)
     orthonormal = jnp.dot(left_prod, inverse.T, precision=highest)
     rank_share = basis.shape[1]
     right_full = jnp.dot(sums[:1024], inverse.T, precision=highest)

time: 1140 us -> 464 us (0.41)
  waiting for transfers between devices: 730 us -> 47.3 us
  Pallas kernels: 112 us -> 341 us
  other arithmetic: 130 us -> 0.56 us
  local copies, waits for them, and re-layouts: 61.5 us -> 17.6 us
  matrix products: 58 us -> 27.4 us
  starting transfers between devices: 13.9 us -> 0.04 us
    all_gather x2 -> x0, waiting for transfers between devices: 421 us -> none  [the longest x1 270 us: per_device(): whole_basis = lax.all_gather(basis.T, 'dp', axis=0, tiled=True).T]
    pallas_call x0 -> x2, Pallas kernels: none -> 228 us  [the longest x1 205 us: merged_and_basis(): pl.pallas_call(grad_kernel, out_shape=(jax.ShapeDtypeStruct((ROWS, 1024),...]
    all_to_all x1 -> x0, waiting for transfers between devices: 217 us -> none  [per_device(): lax.all_to_all(hidden_t, 'dp', split_axis=0, concat_axis=1, tiled=True)]
    another operation x17 -> x0, other arithmetic: 124 us -> none  [the longest x14 80.8 us: per_device(): factor = jnp.linalg.cholesky(gram_sum)]
    psum x1, waiting for transfers between devices: 91.2 us -> 47.3 us  [per_device(): left_prod = lax.psum(jnp.dot(merged, whole_basis, precision=highest), 'mp')]
    unnamed x29 -> x8, local copies, waits for them, and re-layouts: 27.3 us -> 0.96 us
    all_to_all x2 -> x0, local copies, waits for them, and re-layouts: 17.4 us -> none  [per_device(): lax.all_to_all(hidden_t, 'dp', split_axis=0, concat_axis=1, tiled=True)]
    another operation x13 -> x0, matrix products: 15.8 us -> none  [the longest x7 7.98 us: per_device(): jax.scipy.linalg.solve_triangular(factor, jnp.eye(RANK, dtype=jnp.float32...]
  transfers between devices with their start and end apart: 4 -> 1, of which waited for: 4 -> 1; matrix products, arithmetic and copies ran while one was open for 4% -> 0% of each run, Pallas kernels for 0% -> 0%
where the time goes in v2:
time: 464 us; the launch traced here: 458 us
  Pallas kernels  341 us (73%)
  waiting for transfers between devices  47.3 us (10%)
  matrix products  27.4 us (6%)
  local copies, waits for them, and re-layouts  17.6 us (4%)
  between operations  14.4 us (3%)
  blocking collectives  9.41 us (2%)
    pallas_call x1, Pallas kernels, merged_and_basis(): pl.pallas_call(grad_kernel, out_shape=(jax.ShapeDtypeStruct((ROWS, 1024),...  205 us
    pallas_call x1, Pallas kernels, sum_over_dp(): pl.pallas_call(sum_kernel, out_shape=jax.ShapeDtypeStruct(x.shape, f32),...  113 us
    psum x1, waiting for transfers between devices, per_device(): left_prod = lax.psum(jnp.dot(merged, whole_basis, precision=highest), 'mp')  47.3 us
    pallas_call x1, Pallas kernels, inv_factor(): pl.pallas_call(factor_kernel, out_shape=jax.ShapeDtypeStruct((512, 512),...  23 us
    psum x1, blocking collectives, per_device(): squares = lax.psum(jnp.sum(right_full * right_full, axis=0), 'mp')  9.41 us
  transfers between devices with their start and end apart: 1, of which 1 were waited for; matrix products, arithmetic and copies ran while one was open for 0% of the time, Pallas kernels for 0%

profile of v2, /device:TPU:1, one launch (start us, length us, event | category | flops | bytes accessed | tf_op | source)
XLA Modules:
  0.0 457.8 jit_solution(4678200828699720016)
XLA Ops:
  7.2 0.0 all-reduce.3.cloned.1.call-start
  7.2 9.1 %reshape.10 = bf16[64,462,128]{2,1,0:T(8,128)(2,1)} reshape(bf16[29568,128]{1,0:T(8,128)(2,1)} %param.4) | data formatting | bytes 15138816 | tf_op jit(solution)/shard_map/reshape | solution.py:321
  16.3 6.8 %pad.4.hid = bf16[64,480,128]{2,1,0:T(8,128)(2,1)} pad(bf16[64,462,128]{2,1,0:T(8,128)(2,1)} %reshape.10, bf16[]{:T(256)} %constant.3.clone.1), padding=0_0x0_18x0_0 | pad | bytes 15433730 | tf_op jit(solution)/shard_map/jit(_pad)/pad | solution.py:321
  23.2 204.8 %shard_map.67 = (f32[462,1024]{1,0:T(8,128)}, f32[512,1024]{1,0:T(8,128)}) custom-call(bf16[64,480,128]{2,1,0:T(8,128)(2,1)} %pad.4.hid, bf16[128,1024]{1,0:T(8,128)(2,1)} %cot.1, f32[462,1024]{1,0:T(8,128)} %mom.1, f32[8,1024]{1,0:T(8,128)} %bitcast.14), custom_call_target="tpu_custom_call" | custom-call | tf_op jit(solution)/shard_map/pallas_call | solution.py:323
  228.0 0.0 copy-start
  228.1 6.5 %fusion.2 = f32[462,512]{1,0:T(8,128)} fusion(f32[462,1024]{1,0:T(8,128)} %get-tuple-element.5, f32[512,1024]{1,0:T(8,128)} %get-tuple-element.6), kind=kOutput, calls=%fused_computation.9 | convolution fusion | flops 2906652672 | bytes 4935680 | tf_op jit(solution)/shard_map/dot_general | solution.py:415
  234.5 0.0 all-reduce.3.cloned.1.call-update
  234.5 47.3 %all-reduce.3.cloned.1.call-done = f32[462,512]{1,0:T(8,128)} async-done(((f32[462,512]{1,0:T(8,128)}), f32[462,512]{1,0:T(8,128)}) %all-reduce.3.cloned.1.call-update) | async-done | bytes 946192 | tf_op jit(solution)/shard_map/psum | solution.py:415
  281.8 0.0 copy-done
  281.8 0.0 copy-start.2
  281.8 4.9 %fusion.3 = f32[1024,512]{1,0:T(8,128)S(1)} fusion(f32[462,1024]{1,0:T(8,128)S(1)} %copy-done, f32[462,512]{1,0:T(8,128)} %all-reduce.3.cloned.1.call-done), kind=kOutput, calls=%fused_computation.10 | convolution fusion | flops 2906652672 | bytes 4935680 | tf_op jit(solution)/shard_map/dot_general | solution.py:417
  286.7 0.0 copy-done.2
  286.7 2.0 fusion.4
  288.7 0.3 pad_maximum_fusion.in_ref
  289.0 113.3 %shard_map.68 = f32[1536,512]{1,0:T(8,128)S(1)} custom-call(f32[1536,512]{1,0:T(8,128)S(1)} %pad_maximum_fusion.in_ref), custom_call_target="tpu_custom_call" | custom-call | tf_op jit(solution)/shard_map/pallas_call | solution.py:102
  402.3 0.1 slice.6.a
  402.3 23.0 %shard_map.69 = f32[512,512]{1,0:T(8,128)S(1)} custom-call(f32[512,512]{1,0:T(8,128)S(1)} %slice.6.a), custom_call_target="tpu_custom_call" | custom-call | tf_op jit(solution)/shard_map/pallas_call | solution.py:405
  425.4 3.6 multiply_reduce_fusion
  429.0 9.4 %psum.15 = f32[512]{0:T(512)S(1)} all-reduce(f32[512]{0:T(512)S(1)} %get-tuple-element.7), channel_id=1, replica_groups=mesh['dp'=64,'mp'=4] {'mp'}, use_global_device_ids=true, to_apply=%region_2.3 | all-reduce | flops 512 | bytes 4096 | tf_op jit(solution)/shard_map/psum | solution.py:424
  438.4 0.0 copy-start.3
  438.4 0.2 broadcast_divide_fusion
  438.6 0.9 copy-done.3
  439.6 0.0 copy-start.1
  439.6 1.7 fusion.5
  441.3 0.0 copy-done.1
  441.3 4.6 %multiply_subtract_fusion = f32[462,1024]{1,0:T(8,128)} fusion(f32[462,1024]{1,0:T(8,128)S(1)} %copy-done.1, f32[462,512]{1,0:T(8,128)S(1)} %fusion.5, f32[1024,512]{0,1:T(8,128)S(1)} %get-tuple-element.8), kind=kOutput, calls=%fused_computation.5 | convolution fusion | flops 2907598848 | bytes 6828032 | tf_op jit(solution)/shard_map/dot_general | solution.py:429
  445.9 4.2 multiply_convert_fusion
  450.1 0.6 constant_dynamic-slice_fusion
  (1 shorter events, 0.0 us)
Async XLA Ops:
  7.2 274.6 %all-reduce.3.cloned.1.call-start = ((), (), s32[]{:S(2)}) async-start(), calls=%async_computation | async-start | bytes 1900544 | tf_op jit(solution)/shard_map/psum | solution.py:415
  228.0 53.8 %copy-start = (f32[462,1024]{1,0:T(8,128)S(1)}, f32[462,1024]{1,0:T(8,128)}, u32[]{:S(2)}) copy-start(f32[462,1024]{1,0:T(8,128)} %get-tuple-element.5) | copy-start | bytes 5677060
  281.8 4.9 %copy-start.2 = (f32[462,512]{1,0:T(8,128)S(1)}, f32[462,512]{1,0:T(8,128)}, u32[]{:S(2)}) copy-start(f32[462,512]{1,0:T(8,128)} %all-reduce.3.cloned.1.call-done) | copy-start | bytes 2838532
  438.4 1.2 copy-start.3
  439.6 1.7 copy-start.1
Sparse Core Ops, SparseCore 0:
  234.7 47.0 all-reduce.2

commit v3 on v2

v3 whole, which is shorter than its diff:
```python
import jax
import jax.numpy as jnp
from jax import lax
from jax.experimental import pallas as pl
from jax.experimental.pallas import tpu as pltpu
from jax.sharding import PartitionSpec as P

D = 4096
FF = 29568
RANK = 512

NY, NXL, NZ = 4, 2, 8

epsilon = 1e-06
momentum_rate = 0.95


def place():
    dp = lax.axis_index("dp")
    return dp // (NXL * NY), (dp // NY) % NXL, dp % NY


def dp_of(z, xl, y):
    return (z * NXL + xl) * NY + y


def greet(partners):
    barrier = pltpu.get_barrier_semaphore()
    for device in partners:
        pl.semaphore_signal(
            barrier, inc=1, device_id=device, device_id_type=pl.DeviceIdType.MESH
        )
    pl.semaphore_wait(barrier, len(partners))


def send(src, dst, send_sem, recv_sem, device):
    copy = pltpu.make_async_remote_copy(
        src_ref=src,
        dst_ref=dst,
        send_sem=send_sem,
        recv_sem=recv_sem,
        device_id=device,
        device_id_type=pl.DeviceIdType.MESH,
    )
    copy.start()
    return copy


ROWS = 462
HROWS = 480
HALF = HROWS // 2
BLOCKS = 4
BCOLS = 1024 // BLOCKS
N_SEMS = 300


def grad_kernel(
    hid, cot, mom, basis, out, whole, H, za, C, part, came, send_sems, recv_sems, local_sem
):
    z, xl, y = place()
    mp = lax.axis_index("mp")
    xh, core = mp // 2, mp % 2
    z_dev = [{"dp": dp_of((z + k) % NZ, xl, y)} for k in range(NZ)]
    y_dev = [{"dp": dp_of(z, xl, (y + k) % NY)} for k in range(NY)]
    xl_dev = {"dp": dp_of(z, 1 - xl, y)}
    xh_dev = {"mp": (mp + 2) % 4}
    core_dev = {"mp": mp + 1 - 2 * core}
    plane_dev = [
        {"dp": dp_of(z, (xl + i) % NXL, (y + j) % NY)} for i in range(NXL) for j in range(NY)
    ]
    greet(z_dev[1:] + plane_dev[1:] + [xh_dev, core_dev])

    count = iter(range(N_SEMS))
    started = []

    def start(src, dst, device):
        s = next(count)
        copy = send(src, dst, send_sems.at[s], recv_sems.at[s], device)
        started.append(copy)
        return copy

    my_rows = pl.ds(pl.multiple_of(xh * HALF, 16), HALF)
    other_rows = pl.ds(pl.multiple_of((1 - xh) * HALF, 16), HALF)

    def lanes(zs, ys):
        return pl.ds(pl.multiple_of((zs * NY + ys) * 128, 128), 128)

    def group(zs):
        return pl.ds(pl.multiple_of(zs * 512, 512), 512)

    def first_row(d):
        return ROWS * d // 16 * 16 - d // 63 * 16

    shift = ROWS * dp_of(z, xl, y) - first_row(dp_of(z, xl, y))

    def hid_chunk(zd, yd):
        first = first_row(dp_of(zd, core, yd)) + xh * HALF
        return hid.at[pl.ds(pl.multiple_of(first, 16), HALF), :]

    def hidden_task():
        mine = H.at[core, my_rows, lanes(z, y)]
        by_y = {0: [start(hid_chunk(z, (y + j) % NY), mine, y_dev[j]) for j in (1, 3, 2)]}
        by_z, x_copies, c_copies = {}, {}, []
        pairs = [(1, 7), (2, 6), (3, 5), (4,)]

        def send_z(pair):
            for k in pair:
                zd = (z + k) % NZ
                by_z[k] = [start(hid_chunk(zd, y), mine, z_dev[k])] + [
                    start(hid_chunk(zd, (y + j) % NY), za.at[z, j - 1], z_dev[k])
                    for j in (1, 3, 2)
                ]

        def finish(pair):
            for k in pair:
                for copy in by_y[k]:
                    copy.wait_recv()
                ref = H.at[core, my_rows, group((z - k + NZ) % NZ)]
                x_copies[k] = start(ref, ref, xh_dev)
                c_copies.append(start(ref, ref, core_dev))

        def cross(pair):
            for k in pair:
                x_copies[k].wait_recv()
                ref = H.at[core, other_rows, group((z - k + NZ) % NZ)]
                c_copies.append(start(ref, ref, core_dev))

        send_z(pairs[0])
        send_z(pairs[1])
        local = pltpu.make_async_copy(hid_chunk(z, y), mine, local_sem)
        local.start()
        local.wait()
        yield
        seq = [(0,)] + pairs
        for i, pair in enumerate(pairs):
            for k in pair:
                for copy in by_z[k]:
                    copy.wait_recv()
                zs = (z - k + NZ) % NZ
                there = H.at[core, my_rows, lanes(zs, y)]
                by_y[k] = [start(za.at[zs, j - 1], there, y_dev[j]) for j in (1, 3, 2)]
            if i + 2 < len(pairs):
                send_z(pairs[i + 2])
            yield
            finish(seq[i])
            if i:
                cross(seq[i - 1])
            yield
        finish(seq[-1])
        cross(seq[-2])
        yield
        cross(seq[-1])
        yield
        for copy in c_copies:
            copy.wait_recv()

    def shard(b, zs, ys, half=None):
        first = (zs * NY + ys) * 128
        size = 128
        if half is not None:
            first, size = first + half * 64, 64
        return C.at[b, pl.ds(pl.multiple_of(first, 64), size), :]

    def gather_task(b):
        src = cot.at[:, pl.ds(b * BCOLS, BCOLS)]
        mine = shard(b, z, y)
        right, left = start(src, mine, z_dev[1]), start(src, mine, z_dev[NZ - 1])
        pushed = [(z, start(src, mine, y_dev[1]), start(src, mine, y_dev[3]))]
        C[b, pl.ds(pl.multiple_of((z * NY + y) * 128, 128), 128), :] = cot[:, b * BCOLS : (b + 1) * BCOLS]
        last = []

        def forward():
            for zi, up, down in pushed:
                up.wait_recv()
                ref = shard(b, zi, (y + 3) % NY, 0)
                last.append(start(ref, ref, y_dev[1]))
                down.wait_recv()
                ref = shard(b, zi, (y + 1) % NY, 1)
                last.append(start(ref, ref, y_dev[3]))

        for t in range(1, 5):
            yield
            right.wait_recv()
            left.wait_recv()
            low, high = (z - t + NZ) % NZ, (z + t) % NZ
            if t < 4:
                half = (0, 1) if t == 3 else (None, None)
                ref = shard(b, low, y, half[0])
                right = start(ref, ref, z_dev[1])
                ref = shard(b, high, y, half[1])
                left = start(ref, ref, z_dev[NZ - 1])
            now = []
            for zi in (low, high) if t < 4 else (low,):
                ref = shard(b, zi, y)
                now.append((zi, start(ref, ref, y_dev[1]), start(ref, ref, y_dev[3])))
            yield
            forward()
            pushed = now
        yield
        forward()
        yield
        for copy in last:
            copy.wait_recv()

    def basis_task():
        first = pl.multiple_of(dp_of(z, xl, y) * 8, 8)
        mine = whole.at[pl.ds(first, 8), :]
        copies = [start(basis, mine, plane_dev[k]) for k in range(1, 8)]
        whole[pl.ds(first, 8), :] = basis[...]
        yield
        for copy in copies:
            copy.wait_recv()

        def level(zs, half=None):
            at, size = zs * 64, 64
            if half is not None:
                at, size = at + half * 32, 32
            return whole.at[pl.ds(pl.multiple_of(at, 32), size), :]

        right, left = start(level(z), level(z), z_dev[1]), start(level(z), level(z), z_dev[NZ - 1])
        for t in range(1, 5):
            yield
            right.wait_recv()
            left.wait_recv()
            if t < 4:
                half = (0, 1) if t == 3 else (None, None)
                ref = level((z - t + NZ) % NZ, half[0])
                right = start(ref, ref, z_dev[1])
                ref = level((z + t) % NZ, half[1])
                left = start(ref, ref, z_dev[NZ - 1])

    def product(b, rows):
        def step(kk, acc):
            k = pl.ds(pl.multiple_of(kk * 512, 512), 512)
            return acc + jnp.dot(H[rows, :, k], C[b, k, :], preferred_element_type=jnp.float32)

        return lax.fori_loop(0, 8, step, jnp.zeros((HROWS, BCOLS), jnp.float32))

    cross = []

    def aligned(value):
        return pltpu.roll(value, (HROWS - shift) % HROWS, 0)[:ROWS]

    def columns(b):
        return slice(b * BCOLS, (b + 1) * BCOLS)

    def multiply(b):
        part[b] = product(b, 1 - xl)
        cross.append(start(part.at[b], came.at[b], xl_dev))
        turn()
        out[:ROWS, columns(b)] = mom[:, columns(b)] + aligned(product(b, xl))
        out[ROWS:, columns(b)] = jnp.zeros((PAD_ROWS - ROWS, BCOLS), jnp.float32)
        turn()

    def add(b):
        cross[b].wait_recv()
        out[:ROWS, columns(b)] += aligned(came[b])

    gathers = [gather_task(b) for b in range(BLOCKS)]
    hidden = hidden_task()
    running = [gathers[0], hidden, gathers[1]]
    waiting = [gathers[2], gathers[3]]
    for task in running:
        next(task)
    basis_gather = basis_task()

    def turn():
        for task in list(running):
            if next(task, "end") == "end":
                running.remove(task)
                if waiting and task is not hidden:
                    running.append(waiting.pop(0))

    turn()
    next(basis_gather)
    running.append(basis_gather)
    while hidden in running:
        turn()
    for b in range(BLOCKS):
        while gathers[b] in running or gathers[b] in waiting:
            turn()
        multiply(b)
        if b:
            add(b - 1)
    while running:
        turn()
    add(BLOCKS - 1)
    for copy in started:
        copy.wait_send()


def merged_and_basis(hidden_t, cotangent, momentum, basis):
    bf16, f32 = jnp.bfloat16, jnp.float32
    vmem = pl.BlockSpec(memory_space=pltpu.VMEM)
    return pl.pallas_call(
        grad_kernel,
        out_shape=(
            jax.ShapeDtypeStruct((PAD_ROWS, 1024), f32),
            jax.ShapeDtypeStruct((RANK, 1024), f32),
        ),
        in_specs=[pl.BlockSpec(memory_space=pl.ANY), vmem, vmem, vmem],
        out_specs=(vmem, vmem),
        scratch_shapes=[
            pltpu.VMEM((2, HROWS, 4096), bf16),
            pltpu.VMEM((NZ, NY - 1, HALF, 128), bf16),
            pltpu.VMEM((BLOCKS, 4096, BCOLS), bf16),
            pltpu.VMEM((BLOCKS, HROWS, BCOLS), f32),
            pltpu.VMEM((BLOCKS, HROWS, BCOLS), f32),
            pltpu.SemaphoreType.DMA((N_SEMS,)),
            pltpu.SemaphoreType.DMA((N_SEMS,)),
            pltpu.SemaphoreType.DMA,
        ],
        compiler_params=pltpu.CompilerParams(
            collective_id=2, has_side_effects=True, vmem_limit_bytes=56 << 20
        ),
    )(hidden_t, cotangent, momentum, basis.T)


PB = 16

def tdot(a, b):
    return lax.dot_general(a, b, (((0,), (0,)), ((), ())), precision=lax.Precision.HIGHEST, preferred_element_type=jnp.float32)

def eliminate(R0, R1, first):
    n = R0.shape[0]
    row_id = lax.broadcasted_iota(jnp.int32, (n, 128), 0)
    cols = [jnp.broadcast_to(R0[:, first + m : first + m + 1], (n, 128)) for m in range(n)]
    pivots = jnp.ones((n, 128), jnp.float32)
    for j in range(n):
        d = jnp.broadcast_to(cols[j][j : j + 1, :], (n, 128))
        pivots = jnp.where(row_id == j, d, pivots)
        if j + 1 < n:
            f = jnp.where(row_id > j, cols[j], 0.0) * (1.0 / d)
            for m in range(j + 1, n):
                cols[m] = cols[m] - f * cols[m][j : j + 1, :]
            R0 = R0 - f * R0[j : j + 1, :]
            R1 = R1 - f * R1[j : j + 1, :]
    scale = 1.0 / jnp.sqrt(pivots)
    return R0 * scale, R1 * scale

def factor_panel(S, work, p):
    rows = pl.ds(p * 128, 128)
    work[:, :128] = S[rows, p * 128 : p * 128 + 128]
    r = lax.broadcasted_iota(jnp.int32, (128, 128), 0)
    c = lax.broadcasted_iota(jnp.int32, (128, 128), 1)
    work[:, 128:] = jnp.where(r == c, 1.0, 0.0).astype(jnp.float32)
    for b in range(128 // PB):
        lo = b * PB
        u0, u1 = eliminate(work[lo : lo + PB, :128], work[lo : lo + PB, 128:], lo)
        work[lo : lo + PB, 128:] = u1
        if b + 1 < 128 // PB:
            u = jnp.concatenate([u0, u1], axis=1)
            upd = tdot(u0, u)
            work[lo + PB :, :] = work[lo + PB :, :] - upd[lo + PB :, :]

def panel_step(S, work, p):
    factor_panel(S, work, p)
    rows = slice(p * 128, p * 128 + 128)
    end = 512 + (p + 1) * 128
    start = p * 128
    u = jnp.dot(work[:, 128:], S[rows, start:end], precision=lax.Precision.HIGHEST, preferred_element_type=jnp.float32)
    S[rows, start:end] = u
    if p < 3:
        tr = tdot(u[:, 128 : 512 - start], u[:, 128:])
        S[(p + 1) * 128 : 512, start + 128 : end] = S[(p + 1) * 128 : 512, start + 128 : end] - tr

PAD_ROWS = 464
HALF_ROWS = PAD_ROWS // 2
HIGHEST = lax.Precision.HIGHEST


def dot_nt(a, b):
    return lax.dot_general(
        a, b, (((1,), (1,)), ((), ())), precision=HIGHEST, preferred_element_type=jnp.float32
    )


def update_kernel(
    merged, basis, ortho, right, unit,
    lpart, lcame, lown, lxcame, left, gram, gcame, gplane, gz, gsum, gfull, S, work,
    w, wsum, ay, ax, az, ay_acc, ax_acc, cx, cy, cz, cx_acc, cy_acc, sq, sqcame,
    send_sems, recv_sems,
):
    z, xl, y = place()
    mp = lax.axis_index("mp")
    core = mp % 2
    z_dev = [{"dp": dp_of((z + k) % NZ, xl, y)} for k in range(NZ)]
    y_dev = [{"dp": dp_of(z, xl, (y + k) % NY)} for k in range(NY)]
    x_dev = [None, {"dp": dp_of(z, 1 - xl, y)}]
    plane = [((xl + i) % NXL, (y + j) % NY) for i in range(NXL) for j in range(NY)]
    plane_dev = [{"dp": dp_of(z, a, b)} for a, b in plane]
    xh_dev = {"mp": (mp + 2) % 4}
    core_dev = {"mp": mp + 1 - 2 * core}
    far_dev = {"mp": (mp + 2) % 4 + 1 - 2 * core}
    greet(z_dev[1:] + plane_dev[1:] + [xh_dev, core_dev, far_dev])

    count = iter(range(UPDATE_SEMS))
    started = []

    def start(src, dst, device):
        s = next(count)
        copy = send(src, dst, send_sems.at[s], recv_sems.at[s], device)
        started.append(copy)
        return copy

    def rows(first, size):
        return pl.ds(pl.multiple_of(first, 8), size)

    def left_part(half):
        there = rows(half * HALF_ROWS, HALF_ROWS)

        def step(t, _):
            cols = pl.ds(pl.multiple_of(t * 256, 256), 256)
            lpart[there, cols] = dot_nt(merged[there, :], basis[cols, :])
            return 0

        lax.fori_loop(0, 2, step, 0)

    left_part(1 - core)
    swap = start(lpart.at[rows((1 - core) * HALF_ROWS, HALF_ROWS)], lcame, core_dev)
    left_part(core)
    swap.wait_recv()
    mine = rows(core * HALF_ROWS, HALF_ROWS)
    lown[...] = lpart[mine, :] + lcame[...]
    swap = start(lown, lxcame, xh_dev)
    swap.wait_recv()
    left[mine, :] = lown[...] + lxcame[...]
    left_swap = start(left.at[mine], left.at[mine], core_dev)

    def gram_step(t, _):
        cols = pl.ds(pl.multiple_of(t * 128, 128), 128)
        gram[cols, :] = tdot(left[mine, cols], left[mine, :])
        return 0

    lax.fori_loop(0, 4, gram_step, 0)
    swap = start(gram.at[rows((1 - core) * 256, 256)], gcame, core_dev)
    swap.wait_recv()
    gcame[...] = gcame[...] + gram[rows(core * 256, 256), :]
    copies = [
        start(gcame.at[rows((a * NY + b) * 32, 32)], gplane.at[k - 1], plane_dev[k])
        for k, (a, b) in enumerate(plane)
        if k
    ]
    left_swap.wait_recv()

    def w_step(t, _):
        cols = pl.ds(pl.multiple_of(t * 128, 128), 128)
        part = tdot(merged[:, cols], left[...])
        w[0, cols, :] = part[:, :256]
        w[1, cols, :] = part[:, 256:]
        return 0

    lax.fori_loop(0, 8, w_step, 0)

    def sum_task(half, axes):
        source, first, size = w.at[half], 0, 1024
        for n, me, devices, came, acc in axes:
            size = size // n
            pieces = [
                start(source.at[rows(((me + k) % n) * size, size)], came.at[k - 1], devices[k])
                for k in range(1, n)
            ]
            yield
            total = source[rows(me * size, size), :]
            for k in range(n - 1):
                pieces[k].wait_recv()
                total = total + came[k]
            first = first + me * size
            if acc is not None:
                acc[...] = total
                source = acc
        wsum[half, rows(first, size), :] = total
        for n, me, devices, came, acc in reversed(axes):
            ref = wsum.at[half, rows(first, size)]
            pieces = [start(ref, ref, devices[k]) for k in range(1, n)]
            yield
            for copy in pieces:
                copy.wait_recv()
            first = first - me * size
            size = size * n

    y_axis, x_axis, z_axis = (NY, y, y_dev), (NXL, xl, x_dev), (NZ, z, z_dev)
    sums = [
        sum_task(0, [(*y_axis, ay, ay_acc), (*x_axis, ax, ax_acc), (*z_axis, az, None)]),
        sum_task(1, [(*x_axis, cx, cx_acc), (*y_axis, cy, cy_acc), (*z_axis, cz, None)]),
    ]

    def go_on():
        for task in list(sums):
            if next(task, "end") == "end":
                sums.remove(task)

    total = gcame[rows((xl * NY + y) * 32, 32), :]
    for k in range(7):
        copies[k].wait_recv()
        total = total + gplane[k]
    gsum[...] = total

    def z_block(ref, i):
        return ref.at[rows((i // 2) * 8, 8), pl.ds(pl.multiple_of((i % 2) * 256, 256), 256)]

    copies = [
        start(z_block(gsum, (z + k) % NZ), gz.at[k - 1], z_dev[k]) for k in range(1, NZ)
    ]
    go_on()
    my_block = z_block(gsum, z)
    total = my_block[...]
    for k in range(7):
        copies[k].wait_recv()
        total = total + gz[k]
    base = core * 256 + (xl * NY + y) * 32
    here = z_block(gfull.at[rows(base, 32)], z)
    here[...] = total
    copies = [start(here, here, z_dev[k]) for k in range(1, NZ)]
    for copy in copies:
        copy.wait_recv()
    here = gfull.at[rows(base, 32)]
    copies = [start(here, here, plane_dev[k]) for k in range(1, 8)]
    for copy in copies:
        copy.wait_recv()
    here = gfull.at[rows(core * 256, 256)]
    swap = start(here, here, core_dev)
    swap.wait_recv()

    S[:, :512] = gfull[...]
    r = lax.broadcasted_iota(jnp.int32, (512, 512), 0)
    c = lax.broadcasted_iota(jnp.int32, (512, 512), 1)
    S[:, 512:] = jnp.where(r == c, 1.0, 0.0).astype(jnp.float32)
    for p in range(4):
        panel_step(S, work, p)
        go_on()
    while sums:
        go_on()

    def right_step(t, total):
        here = pl.ds(pl.multiple_of(t * 128, 128), 128)
        both = jnp.concatenate([wsum[0, here, :], wsum[1, here, :]], axis=1)
        value = dot_nt(both, S[:, 512:])
        right[here, :] = value
        return total + jnp.sum((value * value).reshape(16, 8, 512), axis=0)

    total = lax.fori_loop(0, 8, right_step, jnp.zeros((8, 512), jnp.float32))
    sq[...] = total
    copies = [
        start(sq, sqcame.at[i], device) for i, device in enumerate([core_dev, xh_dev, far_dev])
    ]

    def ortho_step(t, _):
        here = pl.ds(pl.multiple_of(t * HALF_ROWS, 8), HALF_ROWS)
        ortho[here, :] = dot_nt(left[here, :], S[:, 512:])
        return 0

    lax.fori_loop(0, 2, ortho_step, 0)
    for copy in copies:
        copy.wait_recv()
    squares = jnp.sum(sq[...] + sqcame[0] + sqcame[1] + sqcame[2], axis=0, keepdims=True)
    unit[...] = right[...] * (1.0 / (jnp.sqrt(squares) + epsilon))
    for copy in started:
        copy.wait_send()


UPDATE_SEMS = 100


def low_rank_update(merged, basis_rows):
    f32 = jnp.float32
    vmem = pl.BlockSpec(memory_space=pltpu.VMEM)

    def buffer(*shape):
        return pltpu.VMEM(shape, f32)

    return pl.pallas_call(
        update_kernel,
        out_shape=(
            jax.ShapeDtypeStruct((PAD_ROWS, RANK), f32),
            jax.ShapeDtypeStruct((1024, RANK), f32),
            jax.ShapeDtypeStruct((1024, RANK), f32),
        ),
        in_specs=[vmem, vmem],
        out_specs=(vmem, vmem, vmem),
        scratch_shapes=[
            buffer(PAD_ROWS, RANK),
            buffer(HALF_ROWS, RANK),
            buffer(HALF_ROWS, RANK),
            buffer(HALF_ROWS, RANK),
            buffer(PAD_ROWS, RANK),
            buffer(RANK, RANK),
            buffer(256, RANK),
            buffer(7, 32, RANK),
            buffer(7, 8, 256),
            buffer(32, RANK),
            buffer(RANK, RANK),
            buffer(RANK, 2 * RANK),
            buffer(128, 256),
            buffer(2, 1024, 256),
            buffer(2, 1024, 256),
            buffer(3, 256, 256),
            buffer(1, 128, 256),
            buffer(7, 16, 256),
            buffer(256, 256),
            buffer(128, 256),
            buffer(1, 512, 256),
            buffer(3, 128, 256),
            buffer(7, 16, 256),
            buffer(512, 256),
            buffer(128, 256),
            buffer(8, RANK),
            buffer(3, 8, RANK),
            pltpu.SemaphoreType.DMA((UPDATE_SEMS,)),
            pltpu.SemaphoreType.DMA((UPDATE_SEMS,)),
        ],
        compiler_params=pltpu.CompilerParams(
            collective_id=1, has_side_effects=True, vmem_limit_bytes=50 << 20
        ),
    )(merged, basis_rows)


def per_device(hidden_t, cotangent, momentum, basis):
    high = lax.Precision.HIGH
    merged, basis_rows = merged_and_basis(hidden_t, cotangent, momentum, basis)
    orthonormal, right_full, unit_cols = low_rank_update(merged, basis_rows)
    merged, orthonormal = merged[:ROWS], orthonormal[:ROWS]
    rank_share = basis.shape[1]
    new_basis = lax.dynamic_slice_in_dim(
        unit_cols, lax.axis_index("dp") * rank_share, rank_share, 1
    )
    new_momentum = merged - (1.0 - momentum_rate) * jnp.dot(
        orthonormal, right_full.T, precision=high
    )
    direction_scale = (FF * D / RANK) ** 0.5
    direction = (direction_scale * jnp.dot(orthonormal, unit_cols.T, precision=high)).astype(
        jnp.bfloat16
    )
    return (new_momentum, new_basis, direction)


def solution(mesh):
    in_specs = (P(None, "dp"), P("dp", "mp"), P("dp", "mp"), P("mp", "dp"))
    out_specs = (P("dp", "mp"), P("mp", "dp"), P("dp", "mp"))
    return jax.shard_map(
        per_device, mesh=mesh, in_specs=in_specs, out_specs=out_specs, check_vma=False
    )
```

time: 464 us -> 296 us (0.64); the launches traced: 458 us -> 296 us
  Pallas kernels: 341 us -> 286 us
  waiting for transfers between devices: 47.3 us -> 0 us
  matrix products: 27.4 us -> 7.35 us
  local copies, waits for them, and re-layouts: 17.6 us -> 2.51 us
  between operations: 14.4 us -> 0.67 us
  blocking collectives: 9.41 us -> 0 us
    pallas_call x3 -> x2, Pallas kernels: 341 us -> 286 us  [the longest x1 164 us: merged_and_basis(): pl.pallas_call(grad_kernel, out_shape=(jax.ShapeDtypeStruct((PAD_ROWS, 10...]
    psum x1 -> x0, waiting for transfers between devices: 47.3 us -> none  [per_device(): left_prod = lax.psum(jnp.dot(merged, whole_basis, precision=highest), 'mp')]
    dot_general x7 -> x2, matrix products: 27.4 us -> 7.35 us  [the longest x1 4.7 us: per_device(): jnp.dot(orthonormal, right_full.T, precision=high)]
    psum x1 -> x0, blocking collectives: 9.41 us -> none  [per_device(): squares = lax.psum(jnp.sum(right_full * right_full, axis=0), 'mp')]
    reshape x1 -> x0, local copies, waits for them, and re-layouts: 9.13 us -> none  [merged_and_basis(): hidden_t.reshape(64, ROWS, 128)]
    pad x1 -> x0, local copies, waits for them, and re-layouts: 6.85 us -> none  [merged_and_basis(): jnp.pad(hidden_t.reshape(64, ROWS, 128), ((0, 0), (0, HROWS - ROWS), (0,...]
  transfers between devices with their start and end apart: 1 -> 0, of which waited for: 1 -> 0; matrix products, arithmetic and copies ran while one was open for 0% -> 0% of each run, Pallas kernels for 0% -> 0%
where the time goes in v3:
time: 296 us
  Pallas kernels  286 us (97%)
  matrix products  7.35 us (2%)
    pallas_call x1, Pallas kernels, merged_and_basis(): pl.pallas_call(grad_kernel, out_shape=(jax.ShapeDtypeStruct((PAD_ROWS, 10...  164 us
    pallas_call x1, Pallas kernels, low_rank_update(): pl.pallas_call(update_kernel, out_shape=(jax.ShapeDtypeStruct((PAD_ROWS,...  121 us

profile of v3, /device:TPU:1, one launch (start us, length us, event | category | flops | bytes accessed | tf_op | source)
XLA Modules:
  0.0 296.2 jit_solution(16896351688502136387)
XLA Ops:
  0.6 164.4 %shard_map.67 = (f32[464,1024]{1,0:T(8,128)}, f32[512,1024]{1,0:T(8,128)}) custom-call(bf16[29568,128]{1,0:T(8,128)(2,1)} %hid.1, bf16[128,1024]{1,0:T(8,128)(2,1)} %cot.1, f32[462,1024]{1,0:T(8,128)} %mom.1, f32[8,1024]{1,0:T(8,128)} %bitcast.3), custom_call_target="tpu_custom_call" | custom-call | tf_op jit(solution)/shard_map/pallas_call | solution.py:295
  165.0 0.0 copy-start
  165.0 1.5 copy-done
  166.5 121.3 %shard_map.68 = (f32[464,512]{1,0:T(8,128)S(1)}, f32[1024,512]{1,0:T(8,128)}, f32[1024,512]{1,0:T(8,128)}) custom-call(f32[464,1024]{1,0:T(8,128)S(1)} %copy-done, f32[512,1024]{1,0:T(8,128)} %get-tuple-element.9.basis), custom_call_target="tpu_custom_call" | custom-call | tf_op jit(solution)/shard_map/pallas_call | solution.py:572
  287.8 0.0 copy-start.1
  287.8 4.7 %multiply_subtract_fusion = f32[462,1024]{1,0:T(8,128)} fusion(f32[464,1024]{1,0:T(8,128)S(1)} %copy-done, f32[1024,512]{1,0:T(8,128)} %get-tuple-element.11, f32[464,512]{1,0:T(8,128)S(1)} %get-tuple-element.10), kind=kOutput, calls=%fused_computation.1 | convolution fusion | flops 1454272512 | bytes 6832128 | tf_op jit(solution)/shard_map/dot_general | solution.py:627
  292.6 0.0 copy-done.1
  292.6 2.6 multiply_convert_fusion
  295.2 0.2 constant_dynamic-slice_fusion
  295.4 0.8 copy.7
Async XLA Ops:
  165.0 1.5 copy-start
  287.8 4.7 %copy-start.1 = (f32[1024,512]{1,0:T(8,128)S(1)}, f32[1024,512]{1,0:T(8,128)}, u32[]{:S(2)}) copy-start(f32[1024,512]{1,0:T(8,128)} %get-tuple-element.12) | copy-start | bytes 6291460

commit v4 on v3

--- a/solution.py
+++ b/solution.py
@@ -52,6 +52,7 @@
 BLOCKS = 4
 BCOLS = 1024 // BLOCKS
 N_SEMS = 300
+DEPTH = 2048
 
 
 def grad_kernel(
@@ -231,10 +232,10 @@
 
     def product(b, rows):
         def step(kk, acc):
-            k = pl.ds(pl.multiple_of(kk * 512, 512), 512)
+            k = pl.ds(pl.multiple_of(kk * DEPTH, DEPTH), DEPTH)
             return acc + jnp.dot(H[rows, :, k], C[b, k, :], preferred_element_type=jnp.float32)
 
-        return lax.fori_loop(0, 8, step, jnp.zeros((HROWS, BCOLS), jnp.float32))
+        return lax.fori_loop(0, 4096 // DEPTH, step, jnp.zeros((HROWS, BCOLS), jnp.float32))
 
     cross = []
 
@@ -258,8 +259,7 @@
 
     gathers = [gather_task(b) for b in range(BLOCKS)]
     hidden = hidden_task()
-    running = [gathers[0], hidden, gathers[1]]
-    waiting = [gathers[2], gathers[3]]
+    running = [gathers[0], hidden, *gathers[1:]]
     for task in running:
         next(task)
     basis_gather = basis_task()
@@ -268,8 +268,7 @@
         for task in list(running):
             if next(task, "end") == "end":
                 running.remove(task)
-                if waiting and task is not hidden:
-                    running.append(waiting.pop(0))
+
 
     turn()
     next(basis_gather)
@@ -277,7 +276,7 @@
     while hidden in running:
         turn()
     for b in range(BLOCKS):
-        while gathers[b] in running or gathers[b] in waiting:
+        while gathers[b] in running:
             turn()
         multiply(b)
         if b:
@@ -516,10 +515,12 @@
         copy.wait_recv()
     here = gfull.at[rows(base, 32)]
     copies = [start(here, here, plane_dev[k]) for k in range(1, 8)]
+    go_on()
     for copy in copies:
         copy.wait_recv()
     here = gfull.at[rows(core * 256, 256)]
     swap = start(here, here, core_dev)
+    go_on()
     swap.wait_recv()
 
     S[:, :512] = gfull[...]

time: 296 us -> 297 us (level)
    pallas_call x1, Pallas kernels: 164 us -> 177 us  [merged_and_basis(): pl.pallas_call(grad_kernel, out_shape=(jax.ShapeDtypeStruct((PAD_ROWS, 10...]
    pallas_call x1, Pallas kernels: 121 us -> 109 us  [low_rank_update(): pl.pallas_call(update_kernel, out_shape=(jax.ShapeDtypeStruct((PAD_ROWS,...]
where the time goes in v4:
time: 297 us
  Pallas kernels  286 us (96%)
  matrix products  7.34 us (2%)
    pallas_call x1, Pallas kernels, merged_and_basis(): pl.pallas_call(grad_kernel, out_shape=(jax.ShapeDtypeStruct((PAD_ROWS, 10...  177 us
    pallas_call x1, Pallas kernels, low_rank_update(): pl.pallas_call(update_kernel, out_shape=(jax.ShapeDtypeStruct((PAD_ROWS,...  109 us

profile of v4, /device:TPU:1, one launch (start us, length us, event | category | flops | bytes accessed | tf_op | source)
XLA Modules:
  0.0 297.0 jit_solution(6784610411613117445)
XLA Ops:
  0.6 177.5 %shard_map.67 = (f32[464,1024]{1,0:T(8,128)}, f32[512,1024]{1,0:T(8,128)}) custom-call(bf16[29568,128]{1,0:T(8,128)(2,1)} %hid.1, bf16[128,1024]{1,0:T(8,128)(2,1)} %cot.1, f32[462,1024]{1,0:T(8,128)} %mom.1, f32[8,1024]{1,0:T(8,128)} %bitcast.3), custom_call_target="tpu_custom_call" | custom-call | tf_op jit(solution)/shard_map/pallas_call | solution.py:294
  178.1 0.0 copy-start
  178.1 1.5 copy-done
  179.6 109.0 %shard_map.68 = (f32[464,512]{1,0:T(8,128)S(1)}, f32[1024,512]{1,0:T(8,128)}, f32[1024,512]{1,0:T(8,128)}) custom-call(f32[464,1024]{1,0:T(8,128)S(1)} %copy-done, f32[512,1024]{1,0:T(8,128)} %get-tuple-element.9.basis), custom_call_target="tpu_custom_call" | custom-call | tf_op jit(solution)/shard_map/pallas_call | solution.py:573
  288.6 0.0 copy-start.1
  288.6 4.7 %multiply_subtract_fusion = f32[462,1024]{1,0:T(8,128)} fusion(f32[464,1024]{1,0:T(8,128)S(1)} %copy-done, f32[1024,512]{1,0:T(8,128)} %get-tuple-element.11, f32[464,512]{1,0:T(8,128)S(1)} %get-tuple-element.10), kind=kOutput, calls=%fused_computation.1 | convolution fusion | flops 1454272512 | bytes 6832128 | tf_op jit(solution)/shard_map/dot_general | solution.py:628
  293.3 0.0 copy-done.1
  293.3 2.6 multiply_convert_fusion
  296.0 0.2 constant_dynamic-slice_fusion
  296.2 0.8 copy.7
Async XLA Ops:
  178.1 1.5 copy-start
  288.6 4.7 %copy-start.1 = (f32[1024,512]{1,0:T(8,128)S(1)}, f32[1024,512]{1,0:T(8,128)}, u32[]{:S(2)}) copy-start(f32[1024,512]{1,0:T(8,128)} %get-tuple-element.12) | copy-start | bytes 6291460

commit v5 on v4

--- a/solution.py
+++ b/solution.py
@@ -51,7 +51,7 @@
 HALF = HROWS // 2
 BLOCKS = 4
 BCOLS = 1024 // BLOCKS
-N_SEMS = 300
+N_SEMS = 260
 DEPTH = 2048
 
 
@@ -69,7 +69,8 @@
     plane_dev = [
         {"dp": dp_of(z, (xl + i) % NXL, (y + j) % NY)} for i in range(NXL) for j in range(NY)
     ]
-    greet(z_dev[1:] + plane_dev[1:] + [xh_dev, core_dev])
+    far_dev = {"mp": (mp + 2) % 4 + 1 - 2 * core}
+    greet(z_dev[1:] + plane_dev[1:] + [xh_dev, core_dev, far_dev])
 
     count = iter(range(N_SEMS))
     started = []
@@ -259,7 +260,8 @@
 
     gathers = [gather_task(b) for b in range(BLOCKS)]
     hidden = hidden_task()
-    running = [gathers[0], hidden, *gathers[1:]]
+    running = [gathers[0], hidden, gathers[1]]
+    waiting = [gathers[2], gathers[3]]
     for task in running:
         next(task)
     basis_gather = basis_task()
@@ -268,6 +270,8 @@
         for task in list(running):
             if next(task, "end") == "end":
                 running.remove(task)
+                if waiting and task is not hidden:
+                    running.append(waiting.pop(0))
 
 
     turn()
@@ -276,7 +280,7 @@
     while hidden in running:
         turn()
     for b in range(BLOCKS):
-        while gathers[b] in running:
+        while gathers[b] in running or gathers[b] in waiting:
             turn()
         multiply(b)
         if b:
@@ -286,33 +290,6 @@
     add(BLOCKS - 1)
     for copy in started:
         copy.wait_send()
-
-
-def merged_and_basis(hidden_t, cotangent, momentum, basis):
-    bf16, f32 = jnp.bfloat16, jnp.float32
-    vmem = pl.BlockSpec(memory_space=pltpu.VMEM)
-    return pl.pallas_call(
-        grad_kernel,
-        out_shape=(
-            jax.ShapeDtypeStruct((PAD_ROWS, 1024), f32),
-            jax.ShapeDtypeStruct((RANK, 1024), f32),
-        ),
-        in_specs=[pl.BlockSpec(memory_space=pl.ANY), vmem, vmem, vmem],
-        out_specs=(vmem, vmem),
-        scratch_shapes=[
-            pltpu.VMEM((2, HROWS, 4096), bf16),
-            pltpu.VMEM((NZ, NY - 1, HALF, 128), bf16),
-            pltpu.VMEM((BLOCKS, 4096, BCOLS), bf16),
-            pltpu.VMEM((BLOCKS, HROWS, BCOLS), f32),
-            pltpu.VMEM((BLOCKS, HROWS, BCOLS), f32),
-            pltpu.SemaphoreType.DMA((N_SEMS,)),
-            pltpu.SemaphoreType.DMA((N_SEMS,)),
-            pltpu.SemaphoreType.DMA,
-        ],
-        compiler_params=pltpu.CompilerParams(
-            collective_id=2, has_side_effects=True, vmem_limit_bytes=56 << 20
-        ),
-    )(hidden_t, cotangent, momentum, basis.T)
 
 
 PB = 16
@@ -391,7 +368,6 @@
     xh_dev = {"mp": (mp + 2) % 4}
     core_dev = {"mp": mp + 1 - 2 * core}
     far_dev = {"mp": (mp + 2) % 4 + 1 - 2 * core}
-    greet(z_dev[1:] + plane_dev[1:] + [xh_dev, core_dev, far_dev])
 
     count = iter(range(UPDATE_SEMS))
     started = []
@@ -560,26 +536,44 @@
         copy.wait_send()
 
 
-UPDATE_SEMS = 100
-
-
-def low_rank_update(merged, basis_rows):
-    f32 = jnp.float32
+UPDATE_SEMS = 84
+
+
+GRAD_SCRATCH = 8
+
+
+def whole_kernel(hid, cot, mom, basis, merged, ortho, right, unit, whole, *scratch):
+    grad_kernel(hid, cot, mom, basis, merged, whole, *scratch[:GRAD_SCRATCH])
+    update_kernel(merged, whole, ortho, right, unit, *scratch[GRAD_SCRATCH:])
+
+
+def merge_and_update(hidden_t, cotangent, momentum, basis):
+    bf16, f32 = jnp.bfloat16, jnp.float32
     vmem = pl.BlockSpec(memory_space=pltpu.VMEM)
 
     def buffer(*shape):
         return pltpu.VMEM(shape, f32)
 
     return pl.pallas_call(
-        update_kernel,
+        whole_kernel,
         out_shape=(
+            jax.ShapeDtypeStruct((PAD_ROWS, 1024), f32),
             jax.ShapeDtypeStruct((PAD_ROWS, RANK), f32),
             jax.ShapeDtypeStruct((1024, RANK), f32),
             jax.ShapeDtypeStruct((1024, RANK), f32),
         ),
-        in_specs=[vmem, vmem],
-        out_specs=(vmem, vmem, vmem),
+        in_specs=[pl.BlockSpec(memory_space=pl.ANY), vmem, vmem, vmem],
+        out_specs=(vmem, vmem, vmem, vmem),
         scratch_shapes=[
+            buffer(RANK, 1024),
+            pltpu.VMEM((2, HROWS, 4096), bf16),
+            pltpu.VMEM((NZ, NY - 1, HALF, 128), bf16),
+            pltpu.VMEM((BLOCKS, 4096, BCOLS), bf16),
+            buffer(BLOCKS, HROWS, BCOLS),
+            buffer(BLOCKS, HROWS, BCOLS),
+            pltpu.SemaphoreType.DMA((N_SEMS,)),
+            pltpu.SemaphoreType.DMA((N_SEMS,)),
+            pltpu.SemaphoreType.DMA,
             buffer(PAD_ROWS, RANK),
             buffer(HALF_ROWS, RANK),
             buffer(HALF_ROWS, RANK),
@@ -611,15 +605,16 @@
             pltpu.SemaphoreType.DMA((UPDATE_SEMS,)),
         ],
         compiler_params=pltpu.CompilerParams(
-            collective_id=1, has_side_effects=True, vmem_limit_bytes=50 << 20
+            collective_id=1, has_side_effects=True, vmem_limit_bytes=56 << 20
         ),
-    )(merged, basis_rows)
+    )(hidden_t, cotangent, momentum, basis.T)
 
 
 def per_device(hidden_t, cotangent, momentum, basis):
     high = lax.Precision.HIGH
-    merged, basis_rows = merged_and_basis(hidden_t, cotangent, momentum, basis)
-    orthonormal, right_full, unit_cols = low_rank_update(merged, basis_rows)
+    merged, orthonormal, right_full, unit_cols = merge_and_update(
+        hidden_t, cotangent, momentum, basis
+    )
     merged, orthonormal = merged[:ROWS], orthonormal[:ROWS]
     rank_share = basis.shape[1]
     new_basis = lax.dynamic_slice_in_dim(

time: 297 us -> 279 us (0.939)
  Pallas kernels: 286 us -> 267 us
    pallas_call x2 -> x1, Pallas kernels: 286 us -> 267 us  [merge_and_update(): pl.pallas_call(whole_kernel, out_shape=(jax.ShapeDtypeStruct((PAD_ROWS, 1...]
where the time goes in v5:
time: 279 us; the launch traced here: 278 us
  Pallas kernels  267 us (96%)
  matrix products  8.2 us (3%)
  local copies, waits for them, and re-layouts  2.83 us (1%)
    pallas_call x1, Pallas kernels, merge_and_update(): pl.pallas_call(whole_kernel, out_shape=(jax.ShapeDtypeStruct((PAD_ROWS, 1...  267 us

profile of v5, /device:TPU:1, one launch (start us, length us, event | category | flops | bytes accessed | tf_op | source)
XLA Modules:
  0.0 278.2 jit_solution(11502761123621464682)
XLA Ops:
  0.6 266.5 %shard_map.67 = (f32[464,1024]{1,0:T(8,128)}, f32[464,512]{1,0:T(8,128)}, f32[1024,512]{1,0:T(8,128)}, f32[1024,512]{1,0:T(8,128)}) custom-call(bf16[29568,128]{1,0:T(8,128)(2,1)} %hid.1, bf16[128,1024]{1,0:T(8,128)(2,1)} %cot.1, f32[462,1024]{1,0:T(8,128)} %mom.1, f32[8,1024]{1,0:T(8,128)} %bitcast.3), custom_call_target="tpu_custom_call" | custom-call | tf_op jit(solution)/shard_map/pallas_call | solution.py:557
  267.1 0.0 copy-start.1
  267.1 5.6 %multiply_subtract_fusion = f32[462,1024]{1,0:T(8,128)} fusion(f32[464,1024]{1,0:T(8,128)} %get-tuple-element.7, f32[1024,512]{1,0:T(8,128)} %get-tuple-element.9, f32[464,512]{1,0:T(8,128)} %get-tuple-element.8), kind=kOutput, calls=%fused_computation.1 | convolution fusion | flops 1454272512 | bytes 6832128 | tf_op jit(solution)/shard_map/dot_general | solution.py:623
  272.7 0.0 copy-start
  272.7 0.0 copy-done.1
  272.7 1.0 constant_dynamic-slice_fusion
  273.7 1.8 copy.7
  275.5 0.0 copy-done
  275.5 2.6 multiply_convert_fusion
Async XLA Ops:
  267.1 5.6 %copy-start.1 = (f32[1024,512]{1,0:T(8,128)S(1)}, f32[1024,512]{1,0:T(8,128)}, u32[]{:S(2)}) copy-start(f32[1024,512]{1,0:T(8,128)} %get-tuple-element.10) | copy-start | bytes 6291460
  272.7 2.8 %copy-start = (f32[464,512]{1,0:T(8,128)S(1)}, f32[464,512]{1,0:T(8,128)}, u32[]{:S(2)}) copy-start(f32[464,512]{1,0:T(8,128)} %get-tuple-element.8) | copy-start | bytes 2850820
